TPU v7x, 128 devices: a whole 4x4x4 slice. The times are simulated.
128 devices in a mesh: fsdp: 8 (over z, core), dp: 16 (over y, x).
Axes of the slice: x: 4, y: 4, z: 4, core: 2. Of those that a mesh axis runs over, the one named last changes fastest.
Arguments:
- activations: bfloat16 [2048, 4096], P('dp', 'fsdp'), may hold values from -6 to 6
- out_grads: bfloat16 [2048, 16, 1024], P('dp', 'fsdp'), may hold values from -0.0390625 to 0.0390625
- owners: int32 [8, 16, 1], P('fsdp'), may hold values from 0 to 15; in each aligned block of 16 rows (0 to 15, 16 to 31, ..., all dimensions but the last counted through in order) at most 2 rows name the same one
- left_stats: bfloat16 [8, 32, 1024, 1024], P('fsdp', 'dp'), may hold values from -1 to 2, as said below
- right_stats: bfloat16 [8, 32, 512, 512], P('fsdp', 'dp'), may hold values from -1 to 2, as said below
- left_roots: bfloat16 [8, 32, 1024, 1024], P('fsdp', 'dp'), may hold values from -1 to 1, as said below
- right_roots: bfloat16 [8, 32, 512, 512], P('fsdp', 'dp'), may hold values from -1 to 1, as said below
Outputs:
- new_left_stats: bfloat16 [8, 32, 1024, 1024], P('fsdp', 'dp')
- new_right_stats: bfloat16 [8, 32, 512, 512], P('fsdp', 'dp')
- new_left_roots: bfloat16 [8, 32, 1024, 1024], P('fsdp', 'dp')
- new_right_roots: bfloat16 [8, 32, 512, 512], P('fsdp', 'dp')
- direction: bfloat16 [16, 1024, 4096], P(None, 'dp', 'fsdp')
Inputs may be any that keep to these rules, and one draw needn't show every extreme that they name: `owners`: within each of the 8 rows no value appears more than 2 times, and in some row one value appears exactly 2 times. `left_stats`: each matrix is symmetric and each diagonal entry exceeds the sum of the magnitudes of the other entries of its row. `right_stats`: each matrix is symmetric and each diagonal entry exceeds the sum of the magnitudes of the other entries of its row. `left_roots`: each matrix is symmetric. `right_roots`: each matrix is symmetric.
All inputs are finite; a program needn't handle non-finite values.
Results may differ from a plain program's by a relative error of at most 0.022.
Values may be sent and summed in bfloat16 or wider, within the bound.
No kernel may reach another device: no remote copies, remote signals or barrier semaphores. Data moves between devices by JAX's collectives and lax.ppermute only.
A program may use at most 128 MiB of HBM per device.

v0:
```python
import jax
import jax.numpy as jnp
from jax import lax
from jax.sharding import PartitionSpec as P

DECAY_RATE = 0.95


def newton_root(prev_root, factor):
    square = jnp.dot(prev_root, prev_root, preferred_element_type=jnp.float32).astype(jnp.bfloat16)
    fourth = jnp.dot(square, square, preferred_element_type=jnp.float32).astype(jnp.bfloat16)
    moment = jnp.dot(fourth, factor, preferred_element_type=jnp.float32)
    identity = jnp.eye(factor.shape[0], dtype=jnp.float32)
    newton_step = ((5.0 * identity - moment) * 0.25).astype(jnp.bfloat16)
    return jnp.dot(prev_root, newton_step, preferred_element_type=jnp.float32).astype(jnp.bfloat16)


def gram_rows(block):
    return lax.dot_general(
        block, block, (((1,), (1,)), ((), ())), preferred_element_type=jnp.float32
    )


def gram_cols(block):
    return lax.dot_general(
        block, block, (((0,), (0,)), ((), ())), preferred_element_type=jnp.float32
    )


def slot_ranks(owner_row):
    positions = jnp.arange(owner_row.shape[0])
    same_owner = owner_row[:, None] == owner_row[None, :]
    earlier = positions[None, :] < positions[:, None]
    return jnp.sum(jnp.where(same_owner & earlier, 1, 0), axis=1).astype(jnp.int32)


def update_slot(operands):
    grad_block, left_prev, right_prev, left_root, right_root = operands
    left_new = (
        DECAY_RATE * left_prev.astype(jnp.float32) + (1.0 - DECAY_RATE) * gram_rows(grad_block)
    ).astype(jnp.bfloat16)
    right_new = (
        DECAY_RATE * right_prev.astype(jnp.float32) + (1.0 - DECAY_RATE) * gram_cols(grad_block)
    ).astype(jnp.bfloat16)
    left_next = newton_root(left_root, left_new)
    right_next = newton_root(right_root, right_new)
    half_done = jnp.dot(left_root, grad_block, preferred_element_type=jnp.float32).astype(
        jnp.bfloat16
    )
    result_block = jnp.dot(half_done, right_root, preferred_element_type=jnp.float32).astype(
        jnp.bfloat16
    )
    return (left_new, right_new, left_next, right_next, result_block)


def keep_slot(operands):
    grad_block, left_prev, right_prev, left_root, right_root = operands
    return (left_prev, right_prev, left_root, right_root, jnp.zeros_like(grad_block))


def body(activations, out_grads, owners, left_stats, right_stats, left_roots, right_roots):
    token_count = activations.shape[0]
    block_cols = activations.shape[1]
    block_order = out_grads.shape[2]
    replicas = lax.axis_size("dp")
    strip_rows = block_order // replicas
    slot_count = left_stats.shape[1]
    full_grads = lax.all_gather(out_grads, "fsdp", axis=1, tiled=True)
    row_blocks = full_grads.shape[1]
    owner_row = owners[0, :, 0]
    rank_row = slot_ranks(owner_row)
    owner_match = owner_row[None, None, :] == jnp.arange(replicas, dtype=jnp.int32)[None, :, None]
    rank_match = rank_row[None, None, :] == jnp.arange(slot_count, dtype=jnp.int32)[:, None, None]
    selector = jnp.where(owner_match & rank_match, 1.0, 0.0).astype(jnp.bfloat16)
    grads_ordered = full_grads.reshape(token_count, row_blocks, replicas, strip_rows)
    grads_ordered = grads_ordered.transpose(0, 2, 1, 3).reshape(
        token_count, replicas * row_blocks * strip_rows
    )
    summed = lax.psum_scatter(
        lax.dot_general(
            grads_ordered, activations, (((0,), (0,)), ((), ())), preferred_element_type=jnp.float32
        ).astype(jnp.bfloat16),
        "dp",
        scatter_dimension=0,
        tiled=True,
    )
    strips = summed.reshape(row_blocks, strip_rows, block_cols)
    send_strips = jnp.einsum(
        "mor,rkc->mokc", selector, strips, preferred_element_type=jnp.float32
    ).astype(jnp.bfloat16)
    arrived = lax.all_to_all(send_strips, "dp", split_axis=1, concat_axis=1, tiled=True)
    slot_grads = arrived.reshape(slot_count, block_order, block_cols)
    my_index = lax.axis_index("dp")
    owned_count = jnp.sum(jnp.where(owner_row == my_index, 1, 0))
    left_list, right_list, lroot_list, rroot_list, result_list = ([], [], [], [], [])
    for slot_index in range(slot_count):
        in_use = slot_index < owned_count
        operands = (
            slot_grads[slot_index],
            left_stats[0, slot_index],
            right_stats[0, slot_index],
            left_roots[0, slot_index],
            right_roots[0, slot_index],
        )
        fresh = update_slot(operands)
        stale = keep_slot(operands)
        outcome = tuple(
            (jnp.where(in_use, new_part, old_part) for new_part, old_part in zip(fresh, stale))
        )
        left_list.append(outcome[0])
        right_list.append(outcome[1])
        lroot_list.append(outcome[2])
        rroot_list.append(outcome[3])
        result_list.append(outcome[4])
    results = jnp.stack(result_list).reshape(slot_count, replicas, strip_rows, block_cols)
    returned = lax.all_to_all(results, "dp", split_axis=1, concat_axis=1, tiled=True)
    direction = jnp.einsum(
        "mor,mokc->rkc", selector, returned, preferred_element_type=jnp.float32
    ).astype(jnp.bfloat16)
    return (
        jnp.stack(left_list)[None],
        jnp.stack(right_list)[None],
        jnp.stack(lroot_list)[None],
        jnp.stack(rroot_list)[None],
        direction,
    )


def solution(mesh):
    in_specs = (
        P("dp", "fsdp"),
        P("dp", "fsdp", None),
        P("fsdp", None, None),
        P("fsdp", "dp", None, None),
        P("fsdp", "dp", None, None),
        P("fsdp", "dp", None, None),
        P("fsdp", "dp", None, None),
    )
    out_specs = (
        P("fsdp", "dp", None, None),
        P("fsdp", "dp", None, None),
        P("fsdp", "dp", None, None),
        P("fsdp", "dp", None, None),
        P(None, "dp", "fsdp"),
    )
    return jax.shard_map(body, mesh=mesh, in_specs=in_specs, out_specs=out_specs, check_vma=False)
```

profile of v0, /device:TPU:0, one launch (start us, length us, event | category | flops | bytes accessed | tf_op | source)
XLA Modules:
  0.0 300.5 jit_solution(14094625951148775393)
XLA Ops:
  7.2 0.0 copy-start
  7.2 0.0 all-gather.2.cloned.1.call-start
  7.2 2.0 copy.42
  9.2 0.0 all-gather.2.cloned.1.call-update
  9.2 0.0 reduce-scatter.2.cloned.1.call-start
  9.3 35.9 %all-gather.2.cloned.1.call-done = bf16[128,16,1024]{2,0,1:T(8,128)(2,1)} async-done(((bf16[128,2,1024]{2,0,1:T(8,128)(2,1)}), bf16[128,16,1024]{2,0,1:T(8,128)(2,1)}) %all-gather.2.cloned.1.call-update) | async-done | bytes 4194320 | tf_op jit(solution)/shard_map/all_gather | solution.py:68
  45.1 6.4 %copy.43 = bf16[128,16,1024]{0,2,1:T(8,128)(2,1)} copy(bf16[128,16,1024]{2,0,1:T(8,128)(2,1)} %all-gather.2.cloned.1.call-done) | data formatting | bytes 8388608 | tf_op jit(solution)/shard_map/all_gather | solution.py:68
  51.5 5.6 %copy.44 = bf16[128,16,16,64]{0,3,2,1:T(8,128)(2,1)} copy(bf16[128,16,16,64]{0,3,1,2:T(8,128)(2,1)} %bitcast.184) | data formatting | bytes 8388608 | tf_op jit(solution)/shard_map/transpose | solution.py:76
  57.1 0.0 copy-done
  57.1 10.4 %convolution_convert_fusion = bf16[16384,512]{1,0:T(8,128)(2,1)} fusion(bf16[128,16384]{0,1:T(8,128)(2,1)} %bitcast.183, bf16[128,512]{1,0:T(8,128)(2,1)S(1)} %copy-done), kind=kOutput, calls=%fused_computation | convolution fusion | flops 2155872256 | bytes 21102592 | tf_op jit(solution)/shard_map/dot_general | solution.py:80
  67.5 0.0 copy-start.8
  67.5 0.0 copy-start.9
  67.5 0.0 reduce-scatter.2.cloned.1.call-update
  67.6 0.6 copy-done.8
  68.2 0.6 fusion.137
  70.1 0.1 select_reduce_fusion
  70.2 0.1 iota_compare_fusion.5
  70.3 0.0 copy-done.9
  70.3 1.9 convolution_convert_fusion.6
  72.2 105.8 %reduce-scatter.2.cloned.1.call-done = bf16[1024,512]{1,0:T(8,128)(2,1)} async-done(((bf16[16384,512]{1,0:T(8,128)(2,1)}), bf16[1024,512]{1,0:T(8,128)(2,1)}) %reduce-scatter.2.cloned.1.call-update) | async-done | bytes 1048592 | tf_op jit(solution)/shard_map/reduce_scatter | solution.py:79
  178.0 2.1 convolution_convert_fusion.1
  180.1 2.5 copy.47
  182.6 5.6 %all-to-all-start = ((bf16[2,16,64,512]{3,2,0,1:T(8,128)(2,1)}), bf16[2,16,64,512]{3,2,0,1:T(8,128)(2,1)S(1)}, u32[]{:S(2)}, u32[]{:S(2)}) async-start(bf16[2,16,64,512]{3,2,0,1:T(8,128)(2,1)} %copy.47), calls=%async_computation.1 | async-start | bytes 4194304 | tf_op jit(solution)/shard_map/all_to_all | solution.py:91
  188.2 1.9 convolution_convert_fusion.8
  190.1 11.8 %fusion.26 = bf16[1024,1024]{1,0:T(8,128)(2,1)} fusion(bf16[1,2,1024,1024]{3,2,1,0:T(8,128)(2,1)} %param.12), kind=kOutput, calls=%fused_computation.38 | convolution fusion | flops 4296015872 | bytes 4194304 | tf_op jit(solution)/shard_map/dot_general | solution.py:11
  202.0 11.8 %fusion.32 = bf16[1024,1024]{1,0:T(8,128)(2,1)} fusion(bf16[1,2,1024,1024]{3,2,1,0:T(8,128)(2,1)} %param.12), kind=kOutput, calls=%fused_computation.44 | convolution fusion | flops 4296015872 | bytes 4194304 | tf_op jit(solution)/shard_map/dot_general | solution.py:11
  213.7 0.0 copy-start.4
  213.8 5.9 %all-to-all-done = bf16[2,16,64,512]{3,2,0,1:T(8,128)(2,1)S(1)} async-done(((bf16[2,16,64,512]{3,2,0,1:T(8,128)(2,1)}), bf16[2,16,64,512]{3,2,0,1:T(8,128)(2,1)S(1)}, u32[]{:S(2)}, u32[]{:S(2)}) %all-to-all-start) | async-done | bytes 2097184 | tf_op jit(solution)/shard_map/all_to_all | solution.py:91
  219.7 0.1 fusion.154
  219.8 0.0 copy-start.5
  219.8 0.0 copy-start.7
  219.8 0.0 copy-done.4
  219.8 2.3 fusion.68
  222.1 0.0 copy-start.2
  222.1 2.5 fusion.69
  224.6 0.0 copy-done.5
  224.6 0.0 copy-done.2
  224.6 2.7 add_convert_fusion.1
  227.3 0.0 copy-done.7
  227.3 0.0 copy-start.10
  227.3 2.7 add_convert_fusion
  230.0 0.0 copy-done.10
  230.0 0.0 copy-start.6
  230.0 3.8 %fusion.61 = bf16[1024,512]{1,0:T(8,128)(2,1)S(1)} fusion(pred[]{:T(512)S(6)} %gt.7, bf16[1024,512]{1,0:T(8,128)(2,1)} %bitcast.191, bf16[1,2,1024,1024]{3,2,1,0:T(8,128)(2,1)} %param.12, bf16[1,2,512,512]{3,2,1,0:T(8,128)(2,1)S(1)} %copy-done.10), kind=kOutput, calls=%fused_computation.64 | convolution fusion | flops 1612185600 | bytes 4718593 | tf_op jit(solution)/shard_map/dot_general | solution.py:50
  233.9 0.0 copy-done.6
  233.9 3.5 %fusion.60 = bf16[1024,512]{1,0:T(8,128)(2,1)S(1)} fusion(pred[]{:T(512)S(6)} %gt.6, bf16[1024,512]{1,0:T(8,128)(2,1)S(1)} %bitcast.189, bf16[1,2,1024,1024]{3,2,1,0:T(8,128)(2,1)} %param.12, bf16[1,2,512,512]{3,2,1,0:T(8,128)(2,1)} %param.13), kind=kOutput, calls=%fused_computation.63 | convolution fusion | flops 1612185600 | bytes 4718593 | tf_op jit(solution)/shard_map/dot_general | solution.py:50
  237.4 1.6 fusion.109
  239.0 3.1 %fusion.85 = bf16[1,512,512]{2,1,0:T(8,128)(2,1)} fusion(bf16[512,512]{1,0:T(8,128)(2,1)} %convolution_convert_fusion.6, bf16[512,512]{1,0:T(8,128)(2,1)} %fusion.69, pred[]{:T(512)S(6)} %gt.7, bf16[1,2,512,512]{3,2,1,0:T(8,128)(2,1)} %param.13), kind=kOutput, calls=%fused_computation.88 | convolution fusion | flops 538705920 | bytes 2621441 | tf_op jit(solution)/shard_map/dot_general | solution.py:15
  242.1 3.1 %fusion.82 = bf16[1,512,512]{2,1,0:T(8,128)(2,1)} fusion(bf16[512,512]{1,0:T(8,128)(2,1)} %convolution_convert_fusion.8, bf16[512,512]{1,0:T(8,128)(2,1)} %fusion.68, pred[]{:T(512)S(6)} %gt.6, bf16[1,2,512,512]{3,2,1,0:T(8,128)(2,1)} %param.13), kind=kOutput, calls=%fused_computation.85 | convolution fusion | flops 538705920 | bytes 2621441 | tf_op jit(solution)/shard_map/dot_general | solution.py:15
  245.3 2.0 copy.57
  247.2 2.0 copy.56
  249.2 5.2 %pad_maximum_fusion = bf16[2,16,64,512]{3,0,2,1:T(2,128)(2,1)} fusion(bf16[1,16,64,512]{3,0,2,1:T(2,128)(2,1)S(1)} %copy.57, bf16[1,16,64,512]{3,0,2,1:T(2,128)(2,1)S(1)} %copy.56), kind=kLoop, calls=%fused_computation.14 | loop fusion | flops 4194304 | bytes 4194304 | tf_op jit(solution)/shard_map/stack | solution.py:115
  254.4 3.9 %all-to-all-start.1 = ((bf16[2,16,64,512]{3,0,2,1:T(2,128)(2,1)}), bf16[2,16,64,512]{3,0,2,1:T(2,128)(2,1)S(1)}, u32[]{:S(2)}, u32[]{:S(2)}) async-start(bf16[2,16,64,512]{3,0,2,1:T(2,128)(2,1)} %pad_maximum_fusion), calls=%async_computation.2 | async-start | bytes 4194304 | tf_op jit(solution)/shard_map/all_to_all | solution.py:116
  258.4 9.3 %fusion.8 = bf16[1,1024,1024]{2,1,0:T(8,128)(2,1)} fusion(pred[]{:T(512)S(6)} %gt.7, bf16[1,2,1024,1024]{3,2,1,0:T(8,128)(2,1)} %param.12, bf16[1024,1024]{1,0:T(8,128)(2,1)} %add_convert_fusion, bf16[1024,1024]{1,0:T(8,128)(2,1)} %fusion.26), kind=kOutput, calls=%fused_computation.17 | convolution fusion | flops 4302307328 | bytes 10485761 | tf_op jit(solution)/shard_map/dot_general | solution.py:15
  267.7 0.0 copy-start.3
  267.7 2.9 maximum_bitcast_fusion.2
  270.5 0.0 copy-done.3
  270.5 4.7 %fusion.21 = (bf16[1,1024,1024]{2,1,0:T(8,128)(2,1)}, bf16[1,1024,1024]{2,1,0:T(8,128)(2,1)}) fusion(bf16[1024,1024]{1,0:T(8,128)(2,1)} %add_convert_fusion.1, pred[]{:T(512)S(6)} %gt.6, bf16[1,2,1024,1024]{3,2,1,0:T(8,128)(2,1)S(1)} %copy-done.3, bf16[1024,1024]{1,0:T(8,128)(2,1)} %add_convert_fusion, pred[]{:T(512)S(6)} %gt.7), kind=kLoop, calls=%fused_computation.33 | loop fusion | flops 2097152 | bytes 12582914 | tf_op jit(solution)/shard_map/stack | solution.py:121
  275.3 9.3 %fusion.14 = bf16[1,1024,1024]{2,1,0:T(8,128)(2,1)} fusion(pred[]{:T(512)S(6)} %gt.6, bf16[1,2,1024,1024]{3,2,1,0:T(8,128)(2,1)} %param.12, bf16[1024,1024]{1,0:T(8,128)(2,1)} %add_convert_fusion.1, bf16[1024,1024]{1,0:T(8,128)(2,1)} %fusion.32), kind=kOutput, calls=%fused_computation.24 | convolution fusion | flops 4302307328 | bytes 10485761 | tf_op jit(solution)/shard_map/dot_general | solution.py:15
  284.6 5.9 %maximum_bitcast_fusion = (bf16[1,2,1024,1024]{3,2,1,0:T(8,128)(2,1)}, bf16[1,2,1024,1024]{3,2,1,0:T(8,128)(2,1)}) fusion(bf16[1,1024,1024]{2,1,0:T(8,128)(2,1)} %get-tuple-element.21, bf16[1,1024,1024]{2,1,0:T(8,128)(2,1)} %get-tuple-element.20, bf16[1,1024,1024]{2,1,0:T(8,128)(2,1)} %fusion.8, bf16[1,1024,1024]{2,1,0:T(8,128)(2,1)} %fusion.14), kind=kLoop, calls=%fused_computation.7 | loop fusion | flops 4194304 | bytes 16777216 | tf_op jit(solution)/shard_map/broadcast_in_dim | solution.py:121
  290.5 0.0 all-to-all-done.1
  290.5 1.3 bitcast_convert_fusion
  291.8 1.6 copy.59
  293.4 0.0 copy-done.1
  (2 shorter events, 0.0 us)
Async XLA Ops:
  7.2 49.9 %copy-start = (bf16[128,512]{1,0:T(8,128)(2,1)S(1)}, bf16[128,512]{1,0:T(8,128)(2,1)}, u32[]{:S(2)}) copy-start(bf16[128,512]{1,0:T(8,128)(2,1)} %param.7) | copy-start | bytes 393220
  7.2 38.0 %all-gather.2.cloned.1.call-start = ((), (), s32[]{:S(2)}) async-start(), calls=%async_computation.3 | async-start | bytes 4718592 | tf_op jit(solution)/shard_map/all_gather | solution.py:68
  9.2 168.8 %reduce-scatter.2.cloned.1.call-start = ((), (), s32[]{:S(2)}) async-start(), calls=%async_computation.4 | async-start | bytes 17825792 | tf_op jit(solution)/shard_map/reduce_scatter | solution.py:79
  67.5 0.7 copy-start.8
  67.5 2.8 copy-start.9
  182.6 37.1 %all-to-all-start = ((bf16[2,16,64,512]{3,2,0,1:T(8,128)(2,1)}), bf16[2,16,64,512]{3,2,0,1:T(8,128)(2,1)S(1)}, u32[]{:S(2)}, u32[]{:S(2)}) async-start(bf16[2,16,64,512]{3,2,0,1:T(8,128)(2,1)} %copy.47), calls=%async_computation.1 | async-start | bytes 4194304 | tf_op jit(solution)/shard_map/all_to_all | solution.py:91
  213.7 6.1 %copy-start.4 = (bf16[1,2,512,512]{3,2,1,0:T(8,128)(2,1)S(1)}, bf16[1,2,512,512]{3,2,1,0:T(8,128)(2,1)}, u32[]{:S(2)}) copy-start(bf16[1,2,512,512]{3,2,1,0:T(8,128)(2,1)} %param.11) | copy-start | bytes 3145732
  219.8 4.8 %copy-start.5 = (bf16[1,16,64,512]{3,2,0,1:T(8,128)(2,1)}, bf16[1,16,64,512]{3,2,0,1:T(8,128)(2,1)S(1)}, u32[]{:S(2)}) copy-start(bf16[1,16,64,512]{3,2,0,1:T(8,128)(2,1)S(1)} %get-tuple-element.22) | copy-start | bytes 3145732
  219.8 7.5 %copy-start.7 = (bf16[1,16,64,512]{3,2,0,1:T(8,128)(2,1)}, bf16[1,16,64,512]{3,2,0,1:T(8,128)(2,1)S(1)}, u32[]{:S(2)}) copy-start(bf16[1,16,64,512]{3,2,0,1:T(8,128)(2,1)S(1)} %get-tuple-element.23) | copy-start | bytes 3145732
  222.1 2.5 copy-start.2
  227.3 2.7 copy-start.10
  230.0 3.9 %copy-start.6 = (bf16[1,16,64,512]{3,2,0,1:T(8,128)(2,1)S(1)}, bf16[1,16,64,512]{3,2,0,1:T(8,128)(2,1)}, u32[]{:S(2)}) copy-start(bf16[1,16,64,512]{3,2,0,1:T(8,128)(2,1)} %copy-done.5) | copy-start | bytes 3145732
  254.4 36.1 %all-to-all-start.1 = ((bf16[2,16,64,512]{3,0,2,1:T(2,128)(2,1)}), bf16[2,16,64,512]{3,0,2,1:T(2,128)(2,1)S(1)}, u32[]{:S(2)}, u32[]{:S(2)}) async-start(bf16[2,16,64,512]{3,0,2,1:T(2,128)(2,1)} %pad_maximum_fusion), calls=%async_computation.2 | async-start | bytes 4194304 | tf_op jit(solution)/shard_map/all_to_all | solution.py:116
  267.7 2.9 copy-start.3
  284.6 8.8 %copy-start.1 = (bf16[128,512]{1,0:T(8,128)(2,1)S(1)}, bf16[128,512]{1,0:T(8,128)(2,1)}, u32[]{:S(2)}) copy-start(bf16[128,512]{1,0:T(8,128)(2,1)} %param.7) | copy-start | bytes 393220
Sparse Core Ops, SparseCore 0:
  10.3 34.7 all-gather.1
  67.7 110.2 reduce-scatter.1
where the time goes:
time: 306 us; the launch traced here: 300 us
  waiting for transfers between devices  148 us (48%)
  matrix products  83.6 us (27%)
  local copies, waits for them, and re-layouts  22.7 us (7%)
  other arithmetic  21.2 us (7%)
  between operations  15.7 us (5%)
  starting transfers between devices  9.64 us (3%)
    reduce_scatter x1, waiting for transfers between devices, body(): lax.psum_scatter(lax.dot_general(grads_ordered, activations, (((0,), (0,)...  106 us
    all_gather x1, waiting for transfers between devices, body(): full_grads = lax.all_gather(out_grads, 'fsdp', axis=1, tiled=True)  35.9 us
    dot_general x4, matrix products, newton_root(): jnp.dot(square, square, preferred_element_type=jnp.float32)  27.4 us
    dot_general x4, matrix products, newton_root(): jnp.dot(prev_root, newton_step, preferred_element_type=jnp.float32)  24.9 us
    dot_general x1, matrix products, body(): lax.dot_general(grads_ordered, activations, (((0,), (0,)), ((), ())), pre...  10.4 us
    dot_general x2, matrix products, update_slot(): jnp.dot(half_done, right_root, preferred_element_type=jnp.float32)  7.36 us
    all_gather x1, local copies, waits for them, and re-layouts, body(): full_grads = lax.all_gather(out_grads, 'fsdp', axis=1, tiled=True)  6.38 us
  transfers between devices with their start and end apart: 4, of which 3 were waited for; matrix products, arithmetic and copies ran while one was open for 20% of the time, Pallas kernels for 0%

commit v1 on v0

v1 whole, which is shorter than its diff:
```python
import functools

import jax
import jax.numpy as jnp
from jax import lax
from jax.experimental import pallas as pl
from jax.experimental.pallas import tpu as pltpu
from jax.sharding import Mesh
from jax.sharding import PartitionSpec as P

DECAY_RATE = 0.95
DP = ("y", "x")
FSDP = ("z", "c")
CHUNK = 256
MIB = 1 << 20


def dot(a, b):
    return jnp.dot(a, b, preferred_element_type=jnp.float32)


def params(mib):
    return pltpu.CompilerParams(vmem_limit_bytes=mib * MIB)


def cost(flops, nbytes):
    return pl.CostEstimate(flops=flops, bytes_accessed=nbytes, transcendentals=0)


def rows_loop(total, fn):
    step = min(CHUNK, total)
    for start in range(0, total, step):
        fn(pl.ds(start, step), start)


def powers_kernel(count, left, right, left4, right4, left2, right2):
    @pl.when(pl.program_id(0) < count[0])
    def _():
        for x, sq, out in ((left, left2, left4), (right, right2, right4)):
            order = x.shape[1]

            def square(rows, _, x=x, sq=sq):
                sq[rows] = dot(x[0, rows], x[0]).astype(jnp.bfloat16)

            def fourth(rows, _, sq=sq, out=out):
                out[0, rows] = dot(sq[rows], sq[...]).astype(jnp.bfloat16)

            rows_loop(order, square)
            rows_loop(order, fourth)


def root_powers(count, left, right):
    slots, nl, _ = left.shape
    nr = right.shape[1]
    spec = lambda n: pl.BlockSpec((1, n, n), lambda m, c: (m, 0, 0))
    return pl.pallas_call(
        powers_kernel,
        grid_spec=pltpu.PrefetchScalarGridSpec(
            num_scalar_prefetch=1,
            grid=(slots,),
            in_specs=[spec(nl), spec(nr)],
            out_specs=[spec(nl), spec(nr)],
            scratch_shapes=[pltpu.VMEM((nl, nl), jnp.bfloat16), pltpu.VMEM((nr, nr), jnp.bfloat16)],
        ),
        out_shape=[
            jax.ShapeDtypeStruct(left.shape, jnp.bfloat16),
            jax.ShapeDtypeStruct(right.shape, jnp.bfloat16),
        ],
        compiler_params=params(32),
        cost_estimate=cost(slots * 4 * (nl**3 + nr**3), slots * 4 * (nl**2 + nr**2)),
        name="root_powers",
    )(count, left, right)


def strips_kernel(where, first, acts, *refs):
    planes, out = refs[:-1], refs[-1]
    strip = out.shape[1]
    groups = []
    for z in range(3):
        groups.append(((planes[2 * z],), (planes[2 * z + 1],)))
    groups.append((planes[6:8], planes[8:10]))
    for z, group in enumerate(groups):
        rows = [
            jnp.concatenate([ref[s] for ref in refs_of for s in range(ref.shape[0])], axis=1)
            for refs_of in group
        ]
        g = dot(jnp.concatenate(rows, axis=0), acts[...]).astype(jnp.bfloat16)
        for k in range(2):
            for q in range(2):
                r = first[2 * z + k] + q
                out[where[r]] = g[(2 * k + q) * strip : (2 * k + q + 1) * strip]


def grad_strips(where, first, acts, planes, n_slots, strip):
    tokens, cols = acts.shape
    vmem = pl.BlockSpec(memory_space=pltpu.VMEM)
    smem = pl.BlockSpec(memory_space=pltpu.SMEM)
    rows = sum(p.size for p in planes) // tokens
    return pl.pallas_call(
        strips_kernel,
        in_specs=[smem] * 2 + [vmem] * (1 + len(planes)),
        out_specs=vmem,
        out_shape=jax.ShapeDtypeStruct((n_slots, strip, cols), jnp.bfloat16),
        compiler_params=params(32),
        cost_estimate=cost(2 * rows * tokens * cols, 2 * (rows * tokens + tokens * cols + rows * cols)),
        name="grad_strips",
    )(where, first, acts, *planes)


def direction_kernel(count, grads, left, right, out, half):
    @pl.when(pl.program_id(0) < count[0])
    def _():
        n, cols = left.shape[1], right.shape[1]
        strip = grads.shape[2]
        per = CHUNK // strip
        g = grads[:, 0].reshape(n, cols)

        def rows_of(rows, _):
            half[rows] = dot(left[0, rows], g).astype(jnp.bfloat16)

        rows_loop(n, rows_of)

        for i in range(n // CHUNK):
            d = dot(half[pl.ds(i * CHUNK, CHUNK)], right[0]).astype(jnp.bfloat16)
            out[pl.ds(i * per, per), 0] = d.reshape(per, strip, cols)


def directions(count, grads, left, right):
    replicas, slots, strip, cols = grads.shape
    n = left.shape[1]
    gspec = pl.BlockSpec((replicas, 1, strip, cols), lambda m, c: (0, m, 0, 0))
    spec = lambda k: pl.BlockSpec((1, k, k), lambda m, c: (m, 0, 0))
    return pl.pallas_call(
        direction_kernel,
        grid_spec=pltpu.PrefetchScalarGridSpec(
            num_scalar_prefetch=1,
            grid=(slots,),
            in_specs=[gspec, spec(n), spec(cols)],
            out_specs=gspec,
            scratch_shapes=[pltpu.VMEM((n, cols), jnp.bfloat16)],
        ),
        out_shape=jax.ShapeDtypeStruct(grads.shape, jnp.bfloat16),
        compiler_params=params(32),
        cost_estimate=cost(slots * 2 * n * cols * (n + cols), slots * 2 * (n * n + cols * cols + 2 * n * cols)),
        name="directions",
    )(count, grads, left, right)


def newton(stats, factor4, root, new_stats, step, new_root, gram_rows, ready):
    order = root.shape[0]

    def one_stats(rows, _):
        new_stats[rows] = (
            DECAY_RATE * stats[rows].astype(jnp.float32) + (1.0 - DECAY_RATE) * gram_rows(rows)
        ).astype(jnp.bfloat16)

    def one_step(rows, start):
        moment = dot(factor4[rows], new_stats[...])
        size = moment.shape[0]
        row = lax.broadcasted_iota(jnp.int32, (size, order), 0) + start
        col = lax.broadcasted_iota(jnp.int32, (size, order), 1)
        identity = jnp.where(row == col, 1.0, 0.0)
        step[rows] = ((5.0 * identity - moment) * 0.25).astype(jnp.bfloat16)

    def one_root(rows, _):
        new_root[rows] = dot(root[rows], step[...]).astype(jnp.bfloat16)

    ready(0)
    rows_loop(order, one_stats)
    ready(1)
    rows_loop(order, one_step)
    ready(2)
    rows_loop(order, one_root)


def update_kernel(count, grads, lstats, rstats, lroot, rroot, lfour, rfour, *refs):
    outs, (bl, br, g, ol, orr, lstep, rstep, turned, isems, osems) = refs[:4], refs[4:]
    slots, n = lstats.shape[:2]
    cols = rstats.shape[1]
    strip = grads.shape[2]
    ins = ((lstats, lfour, lroot), (rstats, rfour, rroot))
    held = (bl, br)
    made = (ol, orr)

    def arriving(m, side, i):
        return pltpu.make_async_copy(ins[side][i].at[m], held[side].at[m, i], isems.at[m, side, i])

    def leaving(m, side, i):
        return pltpu.make_async_copy(made[side].at[m, i], outs[2 * i + side].at[m], osems.at[m, side, i])

    def kept(m, side, i):
        return pltpu.make_async_copy(held[side].at[m, 2 * i], outs[2 * i + side].at[m], osems.at[m, side, i])

    def fetch(m):
        for i in range(3):
            for side in range(2):
                arriving(m, side, i).start()

    fetch(0)
    for m in range(slots):
        used = m < count[0]

        @pl.when(used)
        def _(m=m):
            g[...] = grads[:, m].reshape(n, cols)
            turned[...] = g[...].T
            if m + 1 < slots:
                arriving(m, 0, 0).wait()
                fetch(m + 1)

            def left_gram(rows):
                return lax.dot_general(
                    g[rows], g[...], (((1,), (1,)), ((), ())), preferred_element_type=jnp.float32
                )

            def right_gram(rows):
                return dot(turned[rows], g[...])

            for side, gram, step in ((0, left_gram, lstep), (1, right_gram, rstep)):
                stats, four, root = (held[side].at[m, i] for i in range(3))
                newton(
                    stats, four, root, made[side].at[m, 0], step, made[side].at[m, 1], gram,
                    lambda i, side=side: None if m + 1 < slots and (side, i) == (0, 0) else arriving(m, side, i).wait(),
                )
                leaving(m, side, 0).start()
                leaving(m, side, 1).start()

        @pl.when(jnp.logical_not(used))
        def _(m=m):
            for side in range(2):
                for i in range(3):
                    arriving(m, side, i).wait()
                for i in range(2):
                    kept(m, side, i).start()
            if m + 1 < slots:
                fetch(m + 1)

    for m in range(slots):
        for side in range(2):
            for i in range(2):
                leaving(m, side, i).wait()


def update_slots(count, grads, lstats, rstats, lroot, rroot, lfour, rfour):
    replicas, slots, strip, cols = grads.shape
    n = lstats.shape[1]
    smem, vmem, hbm = (pl.BlockSpec(memory_space=k) for k in (pltpu.SMEM, pltpu.VMEM, pl.ANY))
    shape = lambda a: jax.ShapeDtypeStruct(a.shape, jnp.bfloat16)
    return pl.pallas_call(
        update_kernel,
        in_specs=[smem, vmem] + [hbm] * 6,
        out_specs=[hbm] * 4,
        scratch_shapes=[
            pltpu.VMEM((slots, 3, n, n), jnp.bfloat16),
            pltpu.VMEM((slots, 3, cols, cols), jnp.bfloat16),
            pltpu.VMEM((n, cols), jnp.bfloat16),
            pltpu.VMEM((slots, 2, n, n), jnp.bfloat16),
            pltpu.VMEM((slots, 2, cols, cols), jnp.bfloat16),
            pltpu.VMEM((n, n), jnp.bfloat16),
            pltpu.VMEM((cols, cols), jnp.bfloat16),
            pltpu.VMEM((cols, n), jnp.bfloat16),
            pltpu.SemaphoreType.DMA((slots, 2, 3)),
            pltpu.SemaphoreType.DMA((slots, 2, 2)),
        ],
        out_shape=[shape(lstats), shape(rstats), shape(lroot), shape(rroot)],
        compiler_params=params(56),
        cost_estimate=cost(
            slots * (2 * n * n * cols + 2 * n * cols * cols + 4 * (n**3 + cols**3)),
            slots * 2 * (5 * n * n + 5 * cols * cols + n * cols),
        ),
        name="update_slots",
    )(count, grads, lstats, rstats, lroot, rroot, lfour, rfour)


def pick_kernel(where, src, out):
    for r in range(out.shape[0]):
        out[r] = src[where[r]]


def pick(where, returned):
    blocks = where.shape[0]
    shape = (blocks,) + returned.shape[1:]
    vmem = pl.BlockSpec(memory_space=pltpu.VMEM)
    return pl.pallas_call(
        pick_kernel,
        in_specs=[pl.BlockSpec(memory_space=pltpu.SMEM), vmem],
        out_specs=vmem,
        out_shape=jax.ShapeDtypeStruct(shape, returned.dtype),
        compiler_params=params(16),
        cost_estimate=cost(0, 2 * 2 * returned.size),
        name="pick",
    )(where, returned)


def shift(value, axis, by):
    n = lax.axis_size(axis)
    return lax.ppermute(value, axis, [(i, (i + by) % n) for i in range(n)])


def swap_cores(value):
    return lax.ppermute(value, "c", [(0, 1), (1, 0)])


def ring_gather(value, axis):
    return [value] + [shift(value, axis, -k) for k in (1, 2, 3)]


def slot_ranks(owner_row):
    positions = jnp.arange(owner_row.shape[0])
    same_owner = owner_row[:, None] == owner_row[None, :]
    earlier = positions[None, :] < positions[:, None]
    return jnp.sum(jnp.where(same_owner & earlier, 1, 0), axis=1).astype(jnp.int32)


def body(activations, out_grads, owners, left_stats, right_stats, left_roots, right_roots):
    tokens, own_blocks, order = out_grads.shape
    replicas = lax.axis_size("y") * lax.axis_size("x")
    planes, cores = lax.axis_size("z"), lax.axis_size("c")
    strip = order // replicas
    slots = left_stats.shape[1]
    cols = activations.shape[1]

    owner_row = owners[0, :, 0]
    where = owner_row * slots + slot_ranks(owner_row)
    count = jnp.sum(jnp.where(owner_row == lax.axis_index(DP), 1, 0)).astype(jnp.int32).reshape(1)

    turned = out_grads.reshape(tokens, own_blocks, replicas, strip).transpose(2, 1, 3, 0)
    turned = turned.reshape(replicas, own_blocks * strip, tokens)
    own = lax.all_to_all(turned, DP, 0, 0, tiled=True)
    spread = jnp.broadcast_to(activations[None], (replicas,) + activations.shape)
    own, spread = lax.optimization_barrier((own, spread))
    acts = lax.all_to_all(spread, DP, 0, 0, tiled=True)

    down, up = shift(own, "z", 1), shift(own, "z", -1)
    own_too = swap_cores(own)
    h = replicas // 2
    far_lo, far_hi = shift(down[:h], "z", 1), shift(up[h:], "z", -1)
    down_too, up_too = swap_cores(down), swap_cores(up)
    far_lo_too, far_hi_too = swap_cores(far_lo), swap_cores(far_hi)
    pieces = [own, own_too, down, down_too, up, up_too, far_lo, far_hi, far_lo_too, far_hi_too]

    z, c = lax.axis_index("z"), lax.axis_index("c")
    zs = [z, (z + planes - 1) % planes, (z + 1) % planes, (z + 2) % planes]
    first = jnp.stack([(q * cores + k) * own_blocks for q in zs for k in (c, 1 - c)]).astype(jnp.int32)
    strips = grad_strips(where, first, acts.reshape(replicas * tokens, cols), pieces, replicas * slots, strip)
    arrived = lax.all_to_all(strips.reshape(replicas, slots, strip, cols), DP, 0, 0, tiled=True)
    lroots, rroots, _ = lax.optimization_barrier((left_roots[0], right_roots[0], strips))
    lfour, rfour = root_powers(count, lroots, rroots)
    arrived, lfour, rfour = lax.optimization_barrier((arrived, lfour, rfour))
    ready = directions(count, arrived, left_roots[0], right_roots[0])
    returned = lax.all_to_all(ready, DP, 0, 0, tiled=True)
    nls, nrs, nlr, nrr = update_slots(
        count, arrived, left_stats[0], right_stats[0], left_roots[0], right_roots[0], lfour, rfour
    )
    direction = pick(where, returned.reshape(replicas * slots, strip, cols))
    return nls[None], nrs[None], nlr[None], nrr[None], direction


def solution(mesh):
    fsdp, dp = mesh.shape["fsdp"], mesh.shape["dp"]
    torus = Mesh(mesh.devices.reshape(fsdp // 2, 2, dp // 4, 4), ("z", "c", "y", "x"))
    state = P(FSDP, DP, None, None)
    in_specs = (P(DP, FSDP), P(DP, FSDP, None), P(FSDP, None, None), state, state, state, state)
    out_specs = (state, state, state, state, P(None, DP, FSDP))
    return jax.shard_map(body, mesh=torus, in_specs=in_specs, out_specs=out_specs, check_vma=False)
```

time: 306 us -> 140 us (0.46); the launches traced: 300 us -> 142 us
  waiting for transfers between devices: 148 us -> 55.9 us
  matrix products: 83.6 us -> 0 us
  Pallas kernels: 0 us -> 29.3 us
  other arithmetic: 21.2 us -> 0.81 us
  blocking collectives: 0 us -> 18.5 us
  between operations: 15.7 us -> 0.83 us
  starting transfers between devices: 9.64 us -> 21.3 us
  local copies, waits for them, and re-layouts: 22.7 us -> 15.2 us
    reduce_scatter x1 -> x0, waiting for transfers between devices: 106 us -> none  [body(): lax.psum_scatter(lax.dot_general(grads_ordered, activations, (((0,), (0,)...]
    dot_general x17 -> x0, matrix products: 83.6 us -> none  [the longest x4 27.4 us: newton_root(): jnp.dot(square, square, preferred_element_type=jnp.float32)]
    all_gather x1 -> x0, waiting for transfers between devices: 35.9 us -> none  [body(): full_grads = lax.all_gather(out_grads, 'fsdp', axis=1, tiled=True)]
    all_to_all x2 -> x3, waiting for transfers between devices: 5.93 us -> 41 us  [the longest x1 18.4 us: body(): lax.all_to_all(strips.reshape(replicas, slots, strip, cols), DP, 0, 0, ti...]
    pallas_call x0 -> x5, Pallas kernels: none -> 29.3 us  [the longest x1 14.1 us: update_slots(): pl.pallas_call(update_kernel, in_specs=[smem, vmem] + [hbm] * 6, out_spec...]
    all_to_all x0 -> x1, blocking collectives: none -> 18.5 us  [body(): own = lax.all_to_all(turned, DP, 0, 0, tiled=True)]
    ppermute x0 -> x9, waiting for transfers between devices: none -> 14.9 us  [the longest x4 13.9 us: shift(): return lax.ppermute(value, axis, [(i, (i + by) % n) for i in range(n)])]
    another operation x3 -> x0, other arithmetic: 11.6 us -> none  [the longest x1 5.22 us: body(): jnp.stack(result_list).reshape(slot_count, replicas, strip_rows, block_cols)]
  transfers between devices with their start and end apart: 4 -> 12, of which waited for: 3 -> 8; matrix products, arithmetic and copies ran while one was open for 20% -> 1% of each run, Pallas kernels for 0% -> 14%
where the time goes in v1:
time: 140 us; the launch traced here: 142 us
  waiting for transfers between devices  55.9 us (40%)
  Pallas kernels  29.3 us (21%)
  starting transfers between devices  21.3 us (15%)
  blocking collectives  18.5 us (13%)
  local copies, waits for them, and re-layouts  15.2 us (11%)
    all_to_all x1, blocking collectives, body(): own = lax.all_to_all(turned, DP, 0, 0, tiled=True)  18.5 us
    all_to_all x1, waiting for transfers between devices, body(): lax.all_to_all(strips.reshape(replicas, slots, strip, cols), DP, 0, 0, ti...  18.4 us
    all_to_all x1, waiting for transfers between devices, body(): returned = lax.all_to_all(ready, DP, 0, 0, tiled=True)  17.9 us
    pallas_call x1, Pallas kernels, update_slots(): pl.pallas_call(update_kernel, in_specs=[smem, vmem] + [hbm] * 6, out_spec...  14.1 us
    ppermute x4, waiting for transfers between devices, shift(): return lax.ppermute(value, axis, [(i, (i + by) % n) for i in range(n)])  13.9 us
    unnamed x21, local copies, waits for them, and re-layouts  12.6 us
    ppermute x4, starting transfers between devices, shift(): return lax.ppermute(value, axis, [(i, (i + by) % n) for i in range(n)])  7.55 us
    pallas_call x1, Pallas kernels, root_powers(): pl.pallas_call(powers_kernel, grid_spec=pltpu.PrefetchScalarGridSpec(num_...  5.73 us
  transfers between devices with their start and end apart: 12, of which 8 were waited for; matrix products, arithmetic and copies ran while one was open for 1% of the time, Pallas kernels for 14%

profile of v1, /device:TPU:0, one launch (start us, length us, event | category | flops | bytes accessed | tf_op | source)
XLA Modules:
  0.0 141.8 jit_solution(3395389904784681929)
XLA Ops:
  0.6 0.0 copy-start.8
  0.6 1.4 copy.15
  2.1 18.5 %all_to_all.20.refs_0_ = bf16[16,128,128]{2,1,0:T(8,128)(2,1)S(1)} all-to-all(bf16[16,128,128]{2,1,0:T(8,128)(2,1)S(1)} %bitcast.36), channel_id=1, replica_groups=mesh['z'=4,'c'=2,'y'=4,'x'=4] {'y','x'}, dimensions={0} | all-to-all | bytes 1048576 | tf_op jit(solution)/shard_map/all_to_all | solution.py:329
  20.6 0.0 copy-done.8
  20.6 1.5 %broadcast_in_dim.40 = bf16[16,128,512]{2,1,0:T(8,128)(2,1)} broadcast(bf16[128,512]{1,0:T(8,128)(2,1)S(1)} %copy-done.8), dimensions={1,2} | broadcast | bytes 2228224 | tf_op jit(solution)/shard_map/broadcast_in_dim | solution.py:330
  22.1 0.0 copy-start.9
  22.1 3.9 %all-to-all-start.1 = ((bf16[16,128,512]{2,1,0:T(8,128)(2,1)}), bf16[16,128,512]{2,1,0:T(8,128)(2,1)S(1)}, u32[]{:S(2)}, u32[]{:S(2)}) async-start(bf16[16,128,512]{2,1,0:T(8,128)(2,1)} %broadcast_in_dim.40), calls=%async_computation.1 | async-start | bytes 4194304 | tf_op jit(solution)/shard_map/all_to_all | solution.py:332
  25.9 2.0 %collective-permute-start.1 = (bf16[16,128,128]{2,1,0:T(8,128)(2,1)S(1)}, bf16[16,128,128]{2,1,0:T(8,128)(2,1)S(1)}, u32[]{:S(2)}, u32[]{:S(2)}) collective-permute-start(bf16[16,128,128]{2,1,0:T(8,128)(2,1)S(1)} %all_to_all.20.refs_0_), channel_id=1, source_target_pairs={{0,32},{32,64},{64,96},{96,0},{1,33},{33,65},{65,97},{97,1},{2,34}... | collective-permute-start | bytes 1572872 | tf_op jit(solution)/shard_map/ppermute | solution.py:297
  27.9 2.2 %collective-permute-start.3 = (bf16[16,128,128]{2,1,0:T(8,128)(2,1)S(1)}, bf16[16,128,128]{2,1,0:T(8,128)(2,1)}, u32[]{:S(2)}, u32[]{:S(2)}) collective-permute-start(bf16[16,128,128]{2,1,0:T(8,128)(2,1)S(1)} %all_to_all.20.refs_0_), channel_id=1, source_target_pairs={{0,96},{32,0},{64,32},{96,64},{1,97},{33,1},{65,33},{97,65},{2,98}... | collective-permute-start | bytes 1572872 | tf_op jit(solution)/shard_map/ppermute | solution.py:297
  30.1 10.5 %collective-permute-done.1.refs_2_ = bf16[16,128,128]{2,1,0:T(8,128)(2,1)S(1)} collective-permute-done((bf16[16,128,128]{2,1,0:T(8,128)(2,1)S(1)}, bf16[16,128,128]{2,1,0:T(8,128)(2,1)S(1)}, u32[]{:S(2)}, u32[]{:S(2)}) %collective-permute-start.1) | collective-permute-done | bytes 524320 | tf_op jit(solution)/shard_map/ppermute | solution.py:297
  40.7 0.1 collective-permute-start.5
  40.8 0.0 collective-permute-done.3.refs_4_
  40.8 1.0 slice.9
  41.8 3.3 %collective-permute-start.6 = (bf16[8,128,128]{2,1,0:T(8,128)(2,1)S(1)}, bf16[8,128,128]{2,1,0:T(8,128)(2,1)}, u32[]{:S(2)}, u32[]{:S(2)}) collective-permute-start(bf16[8,128,128]{2,1,0:T(8,128)(2,1)S(1)} %slice.9), channel_id=1, source_target_pairs={{0,96},{32,0},{64,32},{96,64},{1,97},{33,1},{65,33},{97,65},{2,98}... | collective-permute-start | bytes 786440 | tf_op jit(solution)/shard_map/ppermute | solution.py:297
  45.0 0.0 collective-permute-start
  45.0 0.5 collective-permute-start.2
  45.6 0.0 collective-permute-start.4
  45.6 2.8 %collective-permute-done.5.refs_6_ = bf16[8,128,128]{2,1,0:T(8,128)(2,1)S(1)} collective-permute-done((bf16[8,128,128]{2,1,0:T(8,128)(2,1)S(1)}, bf16[8,128,128]{2,1,0:T(8,128)(2,1)S(1)}, u32[]{:S(2)}, u32[]{:S(2)}) %collective-permute-start.5) | collective-permute-done | bytes 262176 | tf_op jit(solution)/shard_map/ppermute | solution.py:297
  48.3 0.0 collective-permute-start.7
  48.3 0.6 collective-permute-done.6.refs_7_
  48.9 0.0 collective-permute-start.8
  48.9 0.0 copy-done.9
  48.9 0.2 select_reduce_fusion
  49.2 0.1 stack.35.first
  49.2 0.6 multiply_add_fusion
  49.9 0.0 collective-permute-done.refs_1_
  49.9 0.1 collective-permute-done.7.refs_8_
  50.0 0.8 collective-permute-done.8.refs_9_
  50.8 0.0 collective-permute-done.2.refs_3_
  50.8 0.0 collective-permute-done.4.refs_5_
  50.8 4.7 %all-to-all-done.1 = bf16[16,128,512]{2,1,0:T(8,128)(2,1)S(1)} async-done(((bf16[16,128,512]{2,1,0:T(8,128)(2,1)}), bf16[16,128,512]{2,1,0:T(8,128)(2,1)S(1)}, u32[]{:S(2)}, u32[]{:S(2)}) %all-to-all-start.1) | async-done | bytes 2097184 | tf_op jit(solution)/shard_map/all_to_all | solution.py:332
  55.5 4.1 %grad_strips.1 = bf16[32,64,512]{2,1,0:T(8,128)(2,1)S(1)} custom-call(s32[16]{0:T(128)S(1)} %get-tuple-element.31.where, s32[8]{0:T(128)S(1)} %stack.35.first, bf16[2048,512]{1,0:T(8,128)(2,1)S(1)} %bitcast.27, bf16[16,128,128]{2,1,0:T(8,128)(2,1)S(1)} %all_to_all.20.refs_0_, bf16[16,128,128]{2,1,0:T(8,128)(2,1)} %collective-permute-done.refs_1_, ...), custom_call_target="tpu_custom_call" | custom-call | flops 2147483648 | bytes 7340032 | tf_op jit(solution)/shard_map/grad_strips/pallas_call | solution.py:99
  59.6 0.0 copy-start
  59.6 1.3 copy-done
  60.9 0.0 copy-start.4
  60.9 4.6 %all-to-all-start.2 = ((bf16[16,2,64,512]{3,2,1,0:T(8,128)(2,1)}), bf16[16,2,64,512]{3,2,1,0:T(8,128)(2,1)}, u32[]{:S(2)}, u32[]{:S(2)}) async-start(bf16[16,2,64,512]{3,2,1,0:T(8,128)(2,1)} %bitcast.28), calls=%async_computation.2 | async-start | bytes 4194304 | tf_op jit(solution)/shard_map/all_to_all | solution.py:346
  65.5 0.0 copy-done.4
  65.5 0.0 copy-start.2
  65.5 2.2 %copy-done.2 = bf16[1,2,1024,1024]{3,2,1,0:T(8,128)(2,1)S(1)} copy-done((bf16[1,2,1024,1024]{3,2,1,0:T(8,128)(2,1)S(1)}, bf16[1,2,1024,1024]{3,2,1,0:T(8,128)(2,1)}, u32[]{:S(2)}) %copy-start.2) | copy-done | bytes 4194328
  67.7 5.7 %root_powers.1 = (bf16[2,1024,1024]{2,1,0:T(8,128)(2,1)S(1)}, bf16[2,512,512]{2,1,0:T(8,128)(2,1)S(1)}) custom-call(s32[1]{0:T(128)} %bitcast.1.count, bf16[2,1024,1024]{2,1,0:T(8,128)(2,1)S(1)} %bitcast.31, bf16[2,512,512]{2,1,0:T(8,128)(2,1)S(1)} %bitcast.34), custom_call_target="tpu_custom_call" | custom-call | flops 9663676416 | bytes 10485760 | tf_op jit(solution)/shard_map/root_powers/pallas_call | solution.py:56
  73.4 0.0 copy-start.6
  73.4 1.9 %copy-done.6 = bf16[2,1024,1024]{2,1,0:T(8,128)(2,1)} copy-done((bf16[2,1024,1024]{2,1,0:T(8,128)(2,1)}, bf16[2,1024,1024]{2,1,0:T(8,128)(2,1)S(1)}, u32[]{:S(2)}) %copy-start.6) | copy-done | bytes 4194328
  75.4 0.0 copy-start.7
  75.4 1.0 copy-done.7
  76.3 18.4 %all-to-all-done.2.grads = bf16[16,2,64,512]{3,2,1,0:T(8,128)(2,1)} async-done(((bf16[16,2,64,512]{3,2,1,0:T(8,128)(2,1)}), bf16[16,2,64,512]{3,2,1,0:T(8,128)(2,1)}, u32[]{:S(2)}, u32[]{:S(2)}) %all-to-all-start.2) | async-done | bytes 2097184 | tf_op jit(solution)/shard_map/all_to_all | solution.py:346
  94.7 0.0 copy-start.3
  94.7 2.2 %copy-done.3 = bf16[1,2,1024,1024]{3,2,1,0:T(8,128)(2,1)S(1)} copy-done((bf16[1,2,1024,1024]{3,2,1,0:T(8,128)(2,1)S(1)}, bf16[1,2,1024,1024]{3,2,1,0:T(8,128)(2,1)}, u32[]{:S(2)}) %copy-start.3) | copy-done | bytes 4194328
  96.9 0.0 copy-start.5
  96.9 1.2 copy-done.5
  98.1 3.8 %directions.1 = bf16[16,2,64,512]{3,2,1,0:T(8,128)(2,1)S(1)} custom-call(s32[1]{0:T(128)} %bitcast.1.count, bf16[16,2,64,512]{3,2,1,0:T(8,128)(2,1)} %all-to-all-done.2.grads, bf16[2,1024,1024]{2,1,0:T(8,128)(2,1)S(1)} %bitcast.32, bf16[2,512,512]{2,1,0:T(8,128)(2,1)S(1)} %bitcast.35), custom_call_target="tpu_custom_call" | custom-call | flops 3221225472 | bytes 9437184 | tf_op jit(solution)/shard_map/directions/pallas_call | solution.py:133
  101.9 0.0 copy-start.1
  101.9 1.4 copy-done.1
  103.3 4.8 %all-to-all-start.3 = ((bf16[16,2,64,512]{3,2,1,0:T(8,128)(2,1)}), bf16[16,2,64,512]{3,2,1,0:T(8,128)(2,1)S(1)}, u32[]{:S(2)}, u32[]{:S(2)}) async-start(bf16[16,2,64,512]{3,2,1,0:T(8,128)(2,1)} %copy-done.1), calls=%async_computation.3 | async-start | bytes 4194304 | tf_op jit(solution)/shard_map/all_to_all | solution.py:351
  108.1 14.1 %update_slots.1 = (bf16[2,1024,1024]{2,1,0:T(8,128)(2,1)}, bf16[2,512,512]{2,1,0:T(8,128)(2,1)}, bf16[2,1024,1024]{2,1,0:T(8,128)(2,1)}, bf16[2,512,512]{2,1,0:T(8,128)(2,1)}) custom-call(s32[1]{0:T(128)} %bitcast.1.count, bf16[16,2,64,512]{3,2,1,0:T(8,128)(2,1)} %all-to-all-done.2.grads, bf16[2,1024,1024]{2,1,0:T(8,128)(2,1)} %bitcast.39, ...), custom_call_target="tpu_custom_call" | custom-call | flops 12884901888 | bytes 28311552 | tf_op jit(solution)/shard_map/update_slots/pallas_call | solution.py:249
  122.2 17.9 %all-to-all-done.3 = bf16[16,2,64,512]{3,2,1,0:T(8,128)(2,1)S(1)} async-done(((bf16[16,2,64,512]{3,2,1,0:T(8,128)(2,1)}), bf16[16,2,64,512]{3,2,1,0:T(8,128)(2,1)S(1)}, u32[]{:S(2)}, u32[]{:S(2)}) %all-to-all-start.3) | async-done | bytes 2097184 | tf_op jit(solution)/shard_map/all_to_all | solution.py:351
  140.2 1.6 %pick.1 = bf16[16,64,512]{2,1,0:T(8,128)(2,1)} custom-call(s32[16]{0:T(128)S(1)} %get-tuple-element.31.where, bf16[32,64,512]{2,1,0:T(8,128)(2,1)S(1)} %bitcast.29), custom_call_target="tpu_custom_call" | custom-call | bytes 4194304 | tf_op jit(solution)/shard_map/pick/pallas_call | solution.py:284
  (2 shorter events, 0.1 us)
Async XLA Ops:
  0.6 19.9 %copy-start.8 = (bf16[128,512]{1,0:T(8,128)(2,1)S(1)}, bf16[128,512]{1,0:T(8,128)(2,1)}, u32[]{:S(2)}) copy-start(bf16[128,512]{1,0:T(8,128)(2,1)} %param.7) | copy-start | bytes 393220
  22.1 26.9 %copy-start.9 = (s32[1,16,1]{1,2,0:T(1,128)S(1)}, s32[1,16,1]{1,2,0:T(1,128)}, u32[]{:S(2)}) copy-start(s32[1,16,1]{1,2,0:T(1,128)} %param.9) | copy-start | bytes 196
  22.1 33.4 %all-to-all-start.1 = ((bf16[16,128,512]{2,1,0:T(8,128)(2,1)}), bf16[16,128,512]{2,1,0:T(8,128)(2,1)S(1)}, u32[]{:S(2)}, u32[]{:S(2)}) async-start(bf16[16,128,512]{2,1,0:T(8,128)(2,1)} %broadcast_in_dim.40), calls=%async_computation.1 | async-start | bytes 4194304 | tf_op jit(solution)/shard_map/all_to_all | solution.py:332
  25.9 14.7 %collective-permute-start.1 = (bf16[16,128,128]{2,1,0:T(8,128)(2,1)S(1)}, bf16[16,128,128]{2,1,0:T(8,128)(2,1)S(1)}, u32[]{:S(2)}, u32[]{:S(2)}) collective-permute-start(bf16[16,128,128]{2,1,0:T(8,128)(2,1)S(1)} %all_to_all.20.refs_0_), channel_id=1, source_target_pairs={{0,32},{32,64},{64,96},{96,0},{1,33},{33,65},{65,97},{97,1},{2,34}... | collective-permute-start | bytes 1572872 | tf_op jit(solution)/shard_map/ppermute | solution.py:297
  27.9 12.8 %collective-permute-start.3 = (bf16[16,128,128]{2,1,0:T(8,128)(2,1)S(1)}, bf16[16,128,128]{2,1,0:T(8,128)(2,1)}, u32[]{:S(2)}, u32[]{:S(2)}) collective-permute-start(bf16[16,128,128]{2,1,0:T(8,128)(2,1)S(1)} %all_to_all.20.refs_0_), channel_id=1, source_target_pairs={{0,96},{32,0},{64,32},{96,64},{1,97},{33,1},{65,33},{97,65},{2,98}... | collective-permute-start | bytes 1572872 | tf_op jit(solution)/shard_map/ppermute | solution.py:297
  40.7 7.7 %collective-permute-start.5 = (bf16[8,128,128]{2,1,0:T(8,128)(2,1)S(1)}, bf16[8,128,128]{2,1,0:T(8,128)(2,1)S(1)}, u32[]{:S(2)}, u32[]{:S(2)}) collective-permute-start(bf16[8,128,128]{2,1,0:T(8,128)(2,1)S(1)} %slice.8), channel_id=1, source_target_pairs={{0,32},{32,64},{64,96},{96,0},{1,33},{33,65},{65,97},{97,1},{2,34}... | collective-permute-start | bytes 786440 | tf_op jit(solution)/shard_map/ppermute | solution.py:297
  41.8 7.2 %collective-permute-start.6 = (bf16[8,128,128]{2,1,0:T(8,128)(2,1)S(1)}, bf16[8,128,128]{2,1,0:T(8,128)(2,1)}, u32[]{:S(2)}, u32[]{:S(2)}) collective-permute-start(bf16[8,128,128]{2,1,0:T(8,128)(2,1)S(1)} %slice.9), channel_id=1, source_target_pairs={{0,96},{32,0},{64,32},{96,64},{1,97},{33,1},{65,33},{97,65},{2,98}... | collective-permute-start | bytes 786440 | tf_op jit(solution)/shard_map/ppermute | solution.py:297
  45.0 4.8 %collective-permute-start = (bf16[16,128,128]{2,1,0:T(8,128)(2,1)S(1)}, bf16[16,128,128]{2,1,0:T(8,128)(2,1)}, u32[]{:S(2)}, u32[]{:S(2)}) collective-permute-start(bf16[16,128,128]{2,1,0:T(8,128)(2,1)S(1)} %all_to_all.20.refs_0_), channel_id=1, source_target_pairs={{0,16},{16,0},{1,17},{17,1},{2,18},{18,2},{3,19},{19,3},{4,20},{20... | collective-permute-start | bytes 1572872 | tf_op jit(solution)/shard_map/ppermute | solution.py:301
  45.0 5.8 %collective-permute-start.2 = (bf16[16,128,128]{2,1,0:T(8,128)(2,1)S(1)}, bf16[16,128,128]{2,1,0:T(8,128)(2,1)}, u32[]{:S(2)}, u32[]{:S(2)}) collective-permute-start(bf16[16,128,128]{2,1,0:T(8,128)(2,1)S(1)} %collective-permute-done.1.refs_2_), channel_id=1, source_target_pairs={{0,16},{16,0},{1,17},{17,1},{2,18},{18,2},{3,19},{19,3},{4,20},{20... | collective-permute-start | bytes 1572872 | tf_op jit(solution)/shard_map/ppermute | solution.py:301
  45.6 5.3 %collective-permute-start.4 = (bf16[16,128,128]{2,1,0:T(8,128)(2,1)}, bf16[16,128,128]{2,1,0:T(8,128)(2,1)}, u32[]{:S(2)}, u32[]{:S(2)}) collective-permute-start(bf16[16,128,128]{2,1,0:T(8,128)(2,1)} %collective-permute-done.3.refs_4_), channel_id=1, source_target_pairs={{0,16},{16,0},{1,17},{17,1},{2,18},{18,2},{3,19},{19,3},{4,20},{20... | collective-permute-start | bytes 1572872 | tf_op jit(solution)/shard_map/ppermute | solution.py:301
  48.3 1.7 %collective-permute-start.7 = (bf16[8,128,128]{2,1,0:T(8,128)(2,1)S(1)}, bf16[8,128,128]{2,1,0:T(8,128)(2,1)}, u32[]{:S(2)}, u32[]{:S(2)}) collective-permute-start(bf16[8,128,128]{2,1,0:T(8,128)(2,1)S(1)} %collective-permute-done.5.refs_6_), channel_id=1, source_target_pairs={{0,16},{16,0},{1,17},{17,1},{2,18},{18,2},{3,19},{19,3},{4,20},{20... | collective-permute-start | bytes 786440 | tf_op jit(solution)/shard_map/ppermute | solution.py:301
  48.9 1.9 %collective-permute-start.8 = (bf16[8,128,128]{2,1,0:T(8,128)(2,1)}, bf16[8,128,128]{2,1,0:T(8,128)(2,1)}, u32[]{:S(2)}, u32[]{:S(2)}) collective-permute-start(bf16[8,128,128]{2,1,0:T(8,128)(2,1)} %collective-permute-done.6.refs_7_), channel_id=1, source_target_pairs={{0,16},{16,0},{1,17},{17,1},{2,18},{18,2},{3,19},{19,3},{4,20},{20... | collective-permute-start | bytes 786440 | tf_op jit(solution)/shard_map/ppermute | solution.py:301
  59.6 1.3 copy-start
  60.9 4.6 %copy-start.4 = (bf16[1,2,512,512]{3,2,1,0:T(8,128)(2,1)S(1)}, bf16[1,2,512,512]{3,2,1,0:T(8,128)(2,1)}, u32[]{:S(2)}) copy-start(bf16[1,2,512,512]{3,2,1,0:T(8,128)(2,1)} %param.13) | copy-start | bytes 3145732
  60.9 33.8 %all-to-all-start.2 = ((bf16[16,2,64,512]{3,2,1,0:T(8,128)(2,1)}), bf16[16,2,64,512]{3,2,1,0:T(8,128)(2,1)}, u32[]{:S(2)}, u32[]{:S(2)}) async-start(bf16[16,2,64,512]{3,2,1,0:T(8,128)(2,1)} %bitcast.28), calls=%async_computation.2 | async-start | bytes 4194304 | tf_op jit(solution)/shard_map/all_to_all | solution.py:346
  65.5 2.2 %copy-start.2 = (bf16[1,2,1024,1024]{3,2,1,0:T(8,128)(2,1)S(1)}, bf16[1,2,1024,1024]{3,2,1,0:T(8,128)(2,1)}, u32[]{:S(2)}) copy-start(bf16[1,2,1024,1024]{3,2,1,0:T(8,128)(2,1)} %param.12) | copy-start | bytes 12582916
  73.4 1.9 %copy-start.6 = (bf16[2,1024,1024]{2,1,0:T(8,128)(2,1)}, bf16[2,1024,1024]{2,1,0:T(8,128)(2,1)S(1)}, u32[]{:S(2)}) copy-start(bf16[2,1024,1024]{2,1,0:T(8,128)(2,1)S(1)} %get-tuple-element.25.lfour) | copy-start | bytes 12582916
  75.4 1.0 copy-start.7
  94.7 2.2 %copy-start.3 = (bf16[1,2,1024,1024]{3,2,1,0:T(8,128)(2,1)S(1)}, bf16[1,2,1024,1024]{3,2,1,0:T(8,128)(2,1)}, u32[]{:S(2)}) copy-start(bf16[1,2,1024,1024]{3,2,1,0:T(8,128)(2,1)} %param.12) | copy-start | bytes 12582916
  96.9 1.2 copy-start.5
  101.9 1.4 copy-start.1
  103.3 36.9 %all-to-all-start.3 = ((bf16[16,2,64,512]{3,2,1,0:T(8,128)(2,1)}), bf16[16,2,64,512]{3,2,1,0:T(8,128)(2,1)S(1)}, u32[]{:S(2)}, u32[]{:S(2)}) async-start(bf16[16,2,64,512]{3,2,1,0:T(8,128)(2,1)} %copy-done.1), calls=%async_computation.3 | async-start | bytes 4194304 | tf_op jit(solution)/shard_map/all_to_all | solution.py:351

commit v2 on v1

--- a/solution.py
+++ b/solution.py
@@ -12,6 +12,8 @@
 DP = ("y", "x")
 FSDP = ("z", "c")
 CHUNK = 256
+WHOLE = 1024
+GROUP = 2
 MIB = 1 << 20
 
 
@@ -21,6 +23,10 @@
 
 def params(mib):
     return pltpu.CompilerParams(vmem_limit_bytes=mib * MIB)
+
+
+def in_hbm(*arrays):
+    return [pltpu.with_memory_space_constraint(a, pltpu.HBM) for a in arrays]
 
 
 def cost(flops, nbytes):
@@ -33,62 +39,95 @@
         fn(pl.ds(start, step), start)
 
 
-def powers_kernel(count, left, right, left4, right4, left2, right2):
-    @pl.when(pl.program_id(0) < count[0])
-    def _():
-        for x, sq, out in ((left, left2, left4), (right, right2, right4)):
-            order = x.shape[1]
-
-            def square(rows, _, x=x, sq=sq):
-                sq[rows] = dot(x[0, rows], x[0]).astype(jnp.bfloat16)
-
-            def fourth(rows, _, sq=sq, out=out):
-                out[0, rows] = dot(sq[rows], sq[...]).astype(jnp.bfloat16)
-
-            rows_loop(order, square)
-            rows_loop(order, fourth)
+def powers_kernel(count, left, right, left4, right4, lheld, rheld, lsq, rsq, lout, rout, isems, osems):
+    sides = ((left, lheld, lsq, lout, left4), (right, rheld, rsq, rout, right4))
+
+    def arriving(m, side):
+        x, held = sides[side][:2]
+        return pltpu.make_async_copy(x.at[m], held.at[m], isems.at[m, side])
+
+    def leaving(m, side):
+        return pltpu.make_async_copy(sides[side][3].at[m], sides[side][4].at[m], osems.at[m, side])
+
+    for m in range(left.shape[0]):
+
+        @pl.when(m < count[0])
+        def _(m=m):
+            for side in range(2):
+                arriving(m, side).start()
+
+    for m in range(left.shape[0]):
+
+        @pl.when(m < count[0])
+        def _(m=m):
+            for side, (_, held, sq, out, _) in enumerate(sides):
+                arriving(m, side).wait()
+
+                def square(rows, _):
+                    sq[rows] = dot(held[m, rows], held[m]).astype(jnp.bfloat16)
+
+                def fourth(rows, _):
+                    out[m, rows] = dot(sq[rows], sq[...]).astype(jnp.bfloat16)
+
+                rows_loop(held.shape[1], square)
+                rows_loop(held.shape[1], fourth)
+                leaving(m, side).start()
+
+    for m in range(left.shape[0]):
+
+        @pl.when(m < count[0])
+        def _(m=m):
+            for side in range(2):
+                leaving(m, side).wait()
 
 
 def root_powers(count, left, right):
     slots, nl, _ = left.shape
     nr = right.shape[1]
-    spec = lambda n: pl.BlockSpec((1, n, n), lambda m, c: (m, 0, 0))
+    smem, hbm = pl.BlockSpec(memory_space=pltpu.SMEM), pl.BlockSpec(memory_space=pltpu.HBM)
     return pl.pallas_call(
         powers_kernel,
-        grid_spec=pltpu.PrefetchScalarGridSpec(
-            num_scalar_prefetch=1,
-            grid=(slots,),
-            in_specs=[spec(nl), spec(nr)],
-            out_specs=[spec(nl), spec(nr)],
-            scratch_shapes=[pltpu.VMEM((nl, nl), jnp.bfloat16), pltpu.VMEM((nr, nr), jnp.bfloat16)],
-        ),
-        out_shape=[
-            jax.ShapeDtypeStruct(left.shape, jnp.bfloat16),
-            jax.ShapeDtypeStruct(right.shape, jnp.bfloat16),
+        in_specs=[smem, hbm, hbm],
+        out_specs=[hbm, hbm],
+        scratch_shapes=[
+            pltpu.VMEM(left.shape, jnp.bfloat16),
+            pltpu.VMEM(right.shape, jnp.bfloat16),
+            pltpu.VMEM((nl, nl), jnp.bfloat16),
+            pltpu.VMEM((nr, nr), jnp.bfloat16),
+            pltpu.VMEM(left.shape, jnp.bfloat16),
+            pltpu.VMEM(right.shape, jnp.bfloat16),
+            pltpu.SemaphoreType.DMA((slots, 2)),
+            pltpu.SemaphoreType.DMA((slots, 2)),
         ],
-        compiler_params=params(32),
+        out_shape=[pltpu.HBM(a.shape, jnp.bfloat16) for a in (left, right)],
+        compiler_params=params(24),
         cost_estimate=cost(slots * 4 * (nl**3 + nr**3), slots * 4 * (nl**2 + nr**2)),
         name="root_powers",
-    )(count, left, right)
+    )(count, *in_hbm(left, right))
 
 
 def strips_kernel(where, first, acts, *refs):
-    planes, out = refs[:-1], refs[-1]
+    planes, (out, held, sems) = refs[:-3], refs[-3:]
     strip = out.shape[1]
-    groups = []
-    for z in range(3):
-        groups.append(((planes[2 * z],), (planes[2 * z + 1],)))
+
+    groups = [((planes[2 * z],), (planes[2 * z + 1],)) for z in range(3)]
     groups.append((planes[6:8], planes[8:10]))
-    for z, group in enumerate(groups):
+    copies = []
+    for z in range(0, len(groups), GROUP):
         rows = [
             jnp.concatenate([ref[s] for ref in refs_of for s in range(ref.shape[0])], axis=1)
+            for group in groups[z : z + GROUP]
             for refs_of in group
         ]
         g = dot(jnp.concatenate(rows, axis=0), acts[...]).astype(jnp.bfloat16)
-        for k in range(2):
+        for k in range(2 * GROUP):
             for q in range(2):
-                r = first[2 * z + k] + q
-                out[where[r]] = g[(2 * k + q) * strip : (2 * k + q + 1) * strip]
+                n = 4 * z + 2 * k + q
+                held[n] = g[(2 * k + q) * strip : (2 * k + q + 1) * strip]
+                copies.append(pltpu.make_async_copy(held.at[n], out.at[where[first[2 * z + k] + q]], sems.at[n]))
+                copies[-1].start()
+    for c in copies:
+        c.wait()
 
 
 def grad_strips(where, first, acts, planes, n_slots, strip):
@@ -99,51 +138,88 @@
     return pl.pallas_call(
         strips_kernel,
         in_specs=[smem] * 2 + [vmem] * (1 + len(planes)),
-        out_specs=vmem,
-        out_shape=jax.ShapeDtypeStruct((n_slots, strip, cols), jnp.bfloat16),
+        out_specs=pl.BlockSpec(memory_space=pltpu.HBM),
+        out_shape=pltpu.HBM((n_slots, strip, cols), jnp.bfloat16),
+        scratch_shapes=[
+            pltpu.VMEM((rows // strip, strip, cols), jnp.bfloat16),
+            pltpu.SemaphoreType.DMA((rows // strip,)),
+        ],
         compiler_params=params(32),
         cost_estimate=cost(2 * rows * tokens * cols, 2 * (rows * tokens + tokens * cols + rows * cols)),
         name="grad_strips",
     )(where, first, acts, *planes)
 
 
-def direction_kernel(count, grads, left, right, out, half):
-    @pl.when(pl.program_id(0) < count[0])
-    def _():
-        n, cols = left.shape[1], right.shape[1]
-        strip = grads.shape[2]
-        per = CHUNK // strip
-        g = grads[:, 0].reshape(n, cols)
-
-        def rows_of(rows, _):
-            half[rows] = dot(left[0, rows], g).astype(jnp.bfloat16)
-
-        rows_loop(n, rows_of)
-
-        for i in range(n // CHUNK):
-            d = dot(half[pl.ds(i * CHUNK, CHUNK)], right[0]).astype(jnp.bfloat16)
-            out[pl.ds(i * per, per), 0] = d.reshape(per, strip, cols)
+def direction_kernel(count, grads, left, right, out, lroot, rroot, half, done, lsem, rsem, osem):
+    slots, n = left.shape[:2]
+    cols = right.shape[1]
+    strip = grads.shape[2]
+    per = WHOLE // strip
+    pieces = range(n // WHOLE)
+
+    def rows(m, i):
+        part = pl.ds(i * WHOLE, WHOLE)
+        return pltpu.make_async_copy(left.at[m, part], lroot.at[m, part], lsem.at[m, i])
+
+    def side(m):
+        return pltpu.make_async_copy(right.at[m], rroot.at[m], rsem.at[m])
+
+    def leaving(m, i):
+        part = pl.ds(i * per, per)
+        return pltpu.make_async_copy(done.at[m, part], out.at[part, m], osem.at[m, i])
+
+    def fetch(m):
+        @pl.when(m < count[0])
+        def _():
+            side(m).start()
+            for i in pieces:
+                rows(m, i).start()
+
+    fetch(0)
+    for m in range(slots):
+
+        @pl.when(m < count[0])
+        def _(m=m):
+            side(m).wait()
+            if m + 1 < slots:
+                fetch(m + 1)
+            half[...] = dot(grads[:, m].reshape(n, cols), rroot[m]).astype(jnp.bfloat16)
+            for i in pieces:
+                rows(m, i).wait()
+                d = dot(lroot[m, pl.ds(i * WHOLE, WHOLE)], half[...]).astype(jnp.bfloat16)
+                done[m, pl.ds(i * per, per)] = d.reshape(per, strip, cols)
+                leaving(m, i).start()
+
+    for m in range(slots):
+
+        @pl.when(m < count[0])
+        def _(m=m):
+            for i in pieces:
+                leaving(m, i).wait()
 
 
 def directions(count, grads, left, right):
     replicas, slots, strip, cols = grads.shape
     n = left.shape[1]
-    gspec = pl.BlockSpec((replicas, 1, strip, cols), lambda m, c: (0, m, 0, 0))
-    spec = lambda k: pl.BlockSpec((1, k, k), lambda m, c: (m, 0, 0))
+    smem, vmem, hbm = (pl.BlockSpec(memory_space=k) for k in (pltpu.SMEM, pltpu.VMEM, pltpu.HBM))
     return pl.pallas_call(
         direction_kernel,
-        grid_spec=pltpu.PrefetchScalarGridSpec(
-            num_scalar_prefetch=1,
-            grid=(slots,),
-            in_specs=[gspec, spec(n), spec(cols)],
-            out_specs=gspec,
-            scratch_shapes=[pltpu.VMEM((n, cols), jnp.bfloat16)],
-        ),
-        out_shape=jax.ShapeDtypeStruct(grads.shape, jnp.bfloat16),
-        compiler_params=params(32),
+        in_specs=[smem, vmem, hbm, hbm],
+        out_specs=hbm,
+        scratch_shapes=[
+            pltpu.VMEM((slots, n, n), jnp.bfloat16),
+            pltpu.VMEM((slots, cols, cols), jnp.bfloat16),
+            pltpu.VMEM((n, cols), jnp.bfloat16),
+            pltpu.VMEM((slots, replicas, strip, cols), jnp.bfloat16),
+            pltpu.SemaphoreType.DMA((slots, n // WHOLE)),
+            pltpu.SemaphoreType.DMA((slots,)),
+            pltpu.SemaphoreType.DMA((slots, n // WHOLE)),
+        ],
+        out_shape=pltpu.HBM(grads.shape, jnp.bfloat16),
+        compiler_params=params(24),
         cost_estimate=cost(slots * 2 * n * cols * (n + cols), slots * 2 * (n * n + cols * cols + 2 * n * cols)),
         name="directions",
-    )(count, grads, left, right)
+    )(count, grads, *in_hbm(left, right))
 
 
 def newton(stats, factor4, root, new_stats, step, new_root, gram_rows, ready):
@@ -174,7 +250,7 @@
 
 
 def update_kernel(count, grads, lstats, rstats, lroot, rroot, lfour, rfour, *refs):
-    outs, (bl, br, g, ol, orr, lstep, rstep, turned, isems, osems) = refs[:4], refs[4:]
+    outs, (bl, br, g, ol, orr, lstep, rstep, turned, isems, osems, gsems) = refs[:4], refs[4:]
     slots, n = lstats.shape[:2]
     cols = rstats.shape[1]
     strip = grads.shape[2]
@@ -191,7 +267,11 @@
     def kept(m, side, i):
         return pltpu.make_async_copy(held[side].at[m, 2 * i], outs[2 * i + side].at[m], osems.at[m, side, i])
 
+    def block(m):
+        return pltpu.make_async_copy(grads.at[:, m], g.at[m], gsems.at[m])
+
     def fetch(m):
+        block(m).start()
         for i in range(3):
             for side in range(2):
                 arriving(m, side, i).start()
@@ -202,19 +282,19 @@
 
         @pl.when(used)
         def _(m=m):
-            g[...] = grads[:, m].reshape(n, cols)
-            turned[...] = g[...].T
+            block(m).wait()
+            whole = g[m].reshape(n, cols)
+            turned[...] = whole.T
             if m + 1 < slots:
                 arriving(m, 0, 0).wait()
                 fetch(m + 1)
 
             def left_gram(rows):
-                return lax.dot_general(
-                    g[rows], g[...], (((1,), (1,)), ((), ())), preferred_element_type=jnp.float32
-                )
+                part = g[m, pl.ds(rows.start // strip, rows.size // strip)].reshape(rows.size, cols)
+                return dot(part, turned[...])
 
             def right_gram(rows):
-                return dot(turned[rows], g[...])
+                return dot(turned[rows], g[m].reshape(n, cols))
 
             for side, gram, step in ((0, left_gram, lstep), (1, right_gram, rstep)):
                 stats, four, root = (held[side].at[m, i] for i in range(3))
@@ -227,6 +307,7 @@
 
         @pl.when(jnp.logical_not(used))
         def _(m=m):
+            block(m).wait()
             for side in range(2):
                 for i in range(3):
                     arriving(m, side, i).wait()
@@ -244,16 +325,16 @@
 def update_slots(count, grads, lstats, rstats, lroot, rroot, lfour, rfour):
     replicas, slots, strip, cols = grads.shape
     n = lstats.shape[1]
-    smem, vmem, hbm = (pl.BlockSpec(memory_space=k) for k in (pltpu.SMEM, pltpu.VMEM, pl.ANY))
-    shape = lambda a: jax.ShapeDtypeStruct(a.shape, jnp.bfloat16)
+    smem, hbm = pl.BlockSpec(memory_space=pltpu.SMEM), pl.BlockSpec(memory_space=pltpu.HBM)
+    shape = lambda a: pltpu.HBM(a.shape, jnp.bfloat16)
     return pl.pallas_call(
         update_kernel,
-        in_specs=[smem, vmem] + [hbm] * 6,
+        in_specs=[smem] + [hbm] * 7,
         out_specs=[hbm] * 4,
         scratch_shapes=[
             pltpu.VMEM((slots, 3, n, n), jnp.bfloat16),
             pltpu.VMEM((slots, 3, cols, cols), jnp.bfloat16),
-            pltpu.VMEM((n, cols), jnp.bfloat16),
+            pltpu.VMEM((slots, replicas, strip, cols), jnp.bfloat16),
             pltpu.VMEM((slots, 2, n, n), jnp.bfloat16),
             pltpu.VMEM((slots, 2, cols, cols), jnp.bfloat16),
             pltpu.VMEM((n, n), jnp.bfloat16),
@@ -261,6 +342,7 @@
             pltpu.VMEM((cols, n), jnp.bfloat16),
             pltpu.SemaphoreType.DMA((slots, 2, 3)),
             pltpu.SemaphoreType.DMA((slots, 2, 2)),
+            pltpu.SemaphoreType.DMA((slots,)),
         ],
         out_shape=[shape(lstats), shape(rstats), shape(lroot), shape(rroot)],
         compiler_params=params(56),
@@ -269,23 +351,26 @@
             slots * 2 * (5 * n * n + 5 * cols * cols + n * cols),
         ),
         name="update_slots",
-    )(count, grads, lstats, rstats, lroot, rroot, lfour, rfour)
-
-
-def pick_kernel(where, src, out):
-    for r in range(out.shape[0]):
-        out[r] = src[where[r]]
+    )(count, *in_hbm(grads, lstats, rstats, lroot, rroot, lfour, rfour))
+
+
+def pick_kernel(where, src, out, sems):
+    copies = [pltpu.make_async_copy(src.at[where[r]], out.at[r], sems.at[r]) for r in range(out.shape[0])]
+    for c in copies:
+        c.start()
+    for c in copies:
+        c.wait()
 
 
 def pick(where, returned):
     blocks = where.shape[0]
     shape = (blocks,) + returned.shape[1:]
-    vmem = pl.BlockSpec(memory_space=pltpu.VMEM)
     return pl.pallas_call(
         pick_kernel,
-        in_specs=[pl.BlockSpec(memory_space=pltpu.SMEM), vmem],
-        out_specs=vmem,
-        out_shape=jax.ShapeDtypeStruct(shape, returned.dtype),
+        in_specs=[pl.BlockSpec(memory_space=pltpu.SMEM), pl.BlockSpec(memory_space=pltpu.VMEM)],
+        out_specs=pl.BlockSpec(memory_space=pltpu.HBM),
+        out_shape=pltpu.HBM(shape, returned.dtype),
+        scratch_shapes=[pltpu.SemaphoreType.DMA((blocks,))],
         compiler_params=params(16),
         cost_estimate=cost(0, 2 * 2 * returned.size),
         name="pick",

time: 140 us -> 138 us (0.986); the launches traced: 142 us -> 138 us
  local copies, waits for them, and re-layouts: 15.2 us -> 4.06 us
  Pallas kernels: 29.3 us -> 34.4 us
  waiting for transfers between devices: 55.9 us -> 58.8 us
    unnamed x21 -> x7, local copies, waits for them, and re-layouts: 12.6 us -> 1.42 us
    pallas_call x3, Pallas kernels: 23.6 us -> 27.9 us  [the longest x1 14.7 us: update_slots(): pl.pallas_call(update_kernel, in_specs=[smem] + [hbm] * 7, out_specs=[hbm...]
    all_to_all x1, waiting for transfers between devices: 18.4 us -> 21.8 us  [body(): lax.all_to_all(strips.reshape(replicas, slots, strip, cols), DP, 0, 0, ti...]
  transfers between devices with their start and end apart: 12 -> 12, of which waited for: 8 -> 8; matrix products, arithmetic and copies ran while one was open for 1% -> 1% of each run, Pallas kernels for 14% -> 17%
where the time goes in v2:
time: 138 us
  waiting for transfers between devices  58.8 us (43%)
  Pallas kernels  34.4 us (25%)
  starting transfers between devices  20.4 us (15%)
  blocking collectives  18.5 us (13%)
  local copies, waits for them, and re-layouts  4.06 us (3%)
    all_to_all x1, waiting for transfers between devices, body(): lax.all_to_all(strips.reshape(replicas, slots, strip, cols), DP, 0, 0, ti...  21.8 us
    all_to_all x1, blocking collectives, body(): own = lax.all_to_all(turned, DP, 0, 0, tiled=True)  18.5 us
    all_to_all x1, waiting for transfers between devices, body(): returned = lax.all_to_all(ready, DP, 0, 0, tiled=True)  17.5 us
    pallas_call x1, Pallas kernels, update_slots(): pl.pallas_call(update_kernel, in_specs=[smem] + [hbm] * 7, out_specs=[hbm...  14.7 us
    ppermute x4, waiting for transfers between devices, shift(): return lax.ppermute(value, axis, [(i, (i + by) % n) for i in range(n)])  13.9 us
    pallas_call x1, Pallas kernels, root_powers(): pl.pallas_call(powers_kernel, in_specs=[smem, hbm, hbm], out_specs=[hbm,...  8.37 us
    ppermute x4, starting transfers between devices, shift(): return lax.ppermute(value, axis, [(i, (i + by) % n) for i in range(n)])  7.55 us
    pallas_call x1, Pallas kernels, grad_strips(): pl.pallas_call(strips_kernel, in_specs=[smem] * 2 + [vmem] * (1 + len(pla...  4.88 us
  transfers between devices with their start and end apart: 12, of which 8 were waited for; matrix products, arithmetic and copies ran while one was open for 1% of the time, Pallas kernels for 17%

profile of v2, /device:TPU:0, one launch (start us, length us, event | category | flops | bytes accessed | tf_op | source)
XLA Modules:
  0.0 137.8 jit_solution(10291638862759299213)
XLA Ops:
  0.6 0.0 copy-start.1
  0.6 1.4 %copy.15 = bf16[128,2,1024]{0,2,1:T(8,128)(2,1)S(1)} copy(bf16[128,2,1024]{2,1,0:T(2,128)(2,1)} %param.8) | data formatting | bytes 1048576 | tf_op args[1]
  2.1 18.5 %all_to_all.20.refs_0_ = bf16[16,128,128]{2,1,0:T(8,128)(2,1)S(1)} all-to-all(bf16[16,128,128]{2,1,0:T(8,128)(2,1)S(1)} %bitcast.30), channel_id=1, replica_groups=mesh['z'=4,'c'=2,'y'=4,'x'=4] {'y','x'}, dimensions={0} | all-to-all | bytes 1048576 | tf_op jit(solution)/shard_map/all_to_all | solution.py:414
  20.6 0.0 copy-done.1
  20.6 1.5 %broadcast_in_dim.40 = bf16[16,128,512]{2,1,0:T(8,128)(2,1)} broadcast(bf16[128,512]{1,0:T(8,128)(2,1)S(1)} %copy-done.1), dimensions={1,2} | broadcast | bytes 2228224 | tf_op jit(solution)/shard_map/broadcast_in_dim | solution.py:415
  22.1 0.0 copy-start.2
  22.1 3.9 %all-to-all-start.1 = ((bf16[16,128,512]{2,1,0:T(8,128)(2,1)}), bf16[16,128,512]{2,1,0:T(8,128)(2,1)S(1)}, u32[]{:S(2)}, u32[]{:S(2)}) async-start(bf16[16,128,512]{2,1,0:T(8,128)(2,1)} %broadcast_in_dim.40), calls=%async_computation.1 | async-start | bytes 4194304 | tf_op jit(solution)/shard_map/all_to_all | solution.py:417
  25.9 2.0 %collective-permute-start.1 = (bf16[16,128,128]{2,1,0:T(8,128)(2,1)S(1)}, bf16[16,128,128]{2,1,0:T(8,128)(2,1)S(1)}, u32[]{:S(2)}, u32[]{:S(2)}) collective-permute-start(bf16[16,128,128]{2,1,0:T(8,128)(2,1)S(1)} %all_to_all.20.refs_0_), channel_id=1, source_target_pairs={{0,32},{32,64},{64,96},{96,0},{1,33},{33,65},{65,97},{97,1},{2,34}... | collective-permute-start | bytes 1572872 | tf_op jit(solution)/shard_map/ppermute | solution.py:382
  27.9 2.2 %collective-permute-start.3 = (bf16[16,128,128]{2,1,0:T(8,128)(2,1)S(1)}, bf16[16,128,128]{2,1,0:T(8,128)(2,1)}, u32[]{:S(2)}, u32[]{:S(2)}) collective-permute-start(bf16[16,128,128]{2,1,0:T(8,128)(2,1)S(1)} %all_to_all.20.refs_0_), channel_id=1, source_target_pairs={{0,96},{32,0},{64,32},{96,64},{1,97},{33,1},{65,33},{97,65},{2,98}... | collective-permute-start | bytes 1572872 | tf_op jit(solution)/shard_map/ppermute | solution.py:382
  30.1 10.5 %collective-permute-done.1.refs_2_ = bf16[16,128,128]{2,1,0:T(8,128)(2,1)S(1)} collective-permute-done((bf16[16,128,128]{2,1,0:T(8,128)(2,1)S(1)}, bf16[16,128,128]{2,1,0:T(8,128)(2,1)S(1)}, u32[]{:S(2)}, u32[]{:S(2)}) %collective-permute-start.1) | collective-permute-done | bytes 524320 | tf_op jit(solution)/shard_map/ppermute | solution.py:382
  40.7 0.1 collective-permute-start.5
  40.8 0.0 collective-permute-done.3.refs_4_
  40.8 1.0 slice.9
  41.8 3.3 %collective-permute-start.6 = (bf16[8,128,128]{2,1,0:T(8,128)(2,1)S(1)}, bf16[8,128,128]{2,1,0:T(8,128)(2,1)}, u32[]{:S(2)}, u32[]{:S(2)}) collective-permute-start(bf16[8,128,128]{2,1,0:T(8,128)(2,1)S(1)} %slice.9), channel_id=1, source_target_pairs={{0,96},{32,0},{64,32},{96,64},{1,97},{33,1},{65,33},{97,65},{2,98}... | collective-permute-start | bytes 786440 | tf_op jit(solution)/shard_map/ppermute | solution.py:382
  45.0 0.0 collective-permute-start
  45.0 0.5 collective-permute-start.2
  45.6 0.0 collective-permute-start.4
  45.6 2.8 %collective-permute-done.5.refs_6_ = bf16[8,128,128]{2,1,0:T(8,128)(2,1)S(1)} collective-permute-done((bf16[8,128,128]{2,1,0:T(8,128)(2,1)S(1)}, bf16[8,128,128]{2,1,0:T(8,128)(2,1)S(1)}, u32[]{:S(2)}, u32[]{:S(2)}) %collective-permute-start.5) | collective-permute-done | bytes 262176 | tf_op jit(solution)/shard_map/ppermute | solution.py:382
  48.3 0.0 collective-permute-start.7
  48.3 0.6 collective-permute-done.6.refs_7_
  48.9 0.0 collective-permute-start.8
  48.9 0.0 copy-done.2
  48.9 0.2 select_reduce_fusion
  49.2 0.1 stack.35.first
  49.2 0.7 multiply_add_fusion
  49.9 0.0 collective-permute-done.refs_1_
  49.9 0.1 collective-permute-done.7.refs_8_
  50.0 0.8 collective-permute-done.8.refs_9_
  50.8 0.0 collective-permute-done.2.refs_3_
  50.8 0.0 collective-permute-done.4.refs_5_
  50.8 4.7 %all-to-all-done.1 = bf16[16,128,512]{2,1,0:T(8,128)(2,1)S(1)} async-done(((bf16[16,128,512]{2,1,0:T(8,128)(2,1)}), bf16[16,128,512]{2,1,0:T(8,128)(2,1)S(1)}, u32[]{:S(2)}, u32[]{:S(2)}) %all-to-all-start.1) | async-done | bytes 2097184 | tf_op jit(solution)/shard_map/all_to_all | solution.py:417
  55.5 4.9 %grad_strips.1 = bf16[32,64,512]{2,1,0:T(8,128)(2,1)} custom-call(s32[16]{0:T(128)S(1)} %get-tuple-element.31.where, s32[8]{0:T(128)S(1)} %stack.35.first, bf16[2048,512]{1,0:T(8,128)(2,1)S(1)} %bitcast.27, bf16[16,128,128]{2,1,0:T(8,128)(2,1)S(1)} %all_to_all.20.refs_0_, bf16[16,128,128]{2,1,0:T(8,128)(2,1)} %collective-permute-done.refs_1_, ...), custom_call_target="tpu_custom_call" | custom-call | flops 2147483648 | bytes 7340032 | tf_op jit(solution)/shard_map/grad_strips/pallas_call | solution.py:138
  60.4 3.7 %all-to-all-start.2 = ((bf16[16,2,64,512]{3,2,1,0:T(8,128)(2,1)}), bf16[16,2,64,512]{3,2,1,0:T(8,128)(2,1)S(1)}, u32[]{:S(2)}, u32[]{:S(2)}) async-start(bf16[16,2,64,512]{3,2,1,0:T(8,128)(2,1)} %bitcast.29), calls=%async_computation.2 | async-start | bytes 4194304 | tf_op jit(solution)/shard_map/all_to_all | solution.py:431
  64.1 8.4 %root_powers.1 = (bf16[2,1024,1024]{2,1,0:T(8,128)(2,1)}, bf16[2,512,512]{2,1,0:T(8,128)(2,1)}) custom-call(s32[1]{0:T(128)} %bitcast.1.count, bf16[2,1024,1024]{2,1,0:T(8,128)(2,1)} %bitcast.34, bf16[2,512,512]{2,1,0:T(8,128)(2,1)} %bitcast.38), custom_call_target="tpu_custom_call" | custom-call | flops 9663676416 | bytes 10485760 | tf_op jit(solution)/shard_map/root_powers/pallas_call | solution.py:88
  72.5 21.8 %all-to-all-done.2.grads = bf16[16,2,64,512]{3,2,1,0:T(8,128)(2,1)S(1)} async-done(((bf16[16,2,64,512]{3,2,1,0:T(8,128)(2,1)}), bf16[16,2,64,512]{3,2,1,0:T(8,128)(2,1)S(1)}, u32[]{:S(2)}, u32[]{:S(2)}) %all-to-all-start.2) | async-done | bytes 2097184 | tf_op jit(solution)/shard_map/all_to_all | solution.py:431
  94.3 0.0 copy-start
  94.3 4.8 %directions.1 = bf16[16,2,64,512]{3,2,1,0:T(8,128)(2,1)} custom-call(s32[1]{0:T(128)} %bitcast.1.count, bf16[16,2,64,512]{3,2,1,0:T(8,128)(2,1)S(1)} %all-to-all-done.2.grads, bf16[2,1024,1024]{2,1,0:T(8,128)(2,1)} %bitcast.35, bf16[2,512,512]{2,1,0:T(8,128)(2,1)} %bitcast.39), custom_call_target="tpu_custom_call" | custom-call | flops 3221225472 | bytes 9437184 | tf_op jit(solution)/shard_map/directions/pallas_call | solution.py:205
  99.1 0.0 copy-done
  99.1 4.7 %all-to-all-start.3 = ((bf16[16,2,64,512]{3,2,1,0:T(8,128)(2,1)}), bf16[16,2,64,512]{3,2,1,0:T(8,128)(2,1)S(1)}, u32[]{:S(2)}, u32[]{:S(2)}) async-start(bf16[16,2,64,512]{3,2,1,0:T(8,128)(2,1)} %directions.1), calls=%async_computation.3 | async-start | bytes 4194304 | tf_op jit(solution)/shard_map/all_to_all | solution.py:436
  103.8 14.7 %update_slots.1 = (bf16[2,1024,1024]{2,1,0:T(8,128)(2,1)}, bf16[2,512,512]{2,1,0:T(8,128)(2,1)}, bf16[2,1024,1024]{2,1,0:T(8,128)(2,1)}, bf16[2,512,512]{2,1,0:T(8,128)(2,1)}) custom-call(s32[1]{0:T(128)} %bitcast.1.count, bf16[16,2,64,512]{3,2,1,0:T(8,128)(2,1)} %copy-done, bf16[2,1024,1024]{2,1,0:T(8,128)(2,1)} %bitcast.33, bf16[2,512,512]{2,1,0:T(8,128)(2,1)} %bitcast.37, ...), custom_call_target="tpu_custom_call" | custom-call | flops 12884901888 | bytes 28311552 | tf_op jit(solution)/shard_map/update_slots/pallas_call | solution.py:330
  118.6 17.5 %all-to-all-done.3 = bf16[16,2,64,512]{3,2,1,0:T(8,128)(2,1)S(1)} async-done(((bf16[16,2,64,512]{3,2,1,0:T(8,128)(2,1)}), bf16[16,2,64,512]{3,2,1,0:T(8,128)(2,1)S(1)}, u32[]{:S(2)}, u32[]{:S(2)}) %all-to-all-start.3) | async-done | bytes 2097184 | tf_op jit(solution)/shard_map/all_to_all | solution.py:436
  136.0 1.6 %pick.1 = bf16[16,64,512]{2,1,0:T(8,128)(2,1)} custom-call(s32[16]{0:T(128)S(1)} %get-tuple-element.31.where, bf16[32,64,512]{2,1,0:T(8,128)(2,1)S(1)} %bitcast.28), custom_call_target="tpu_custom_call" | custom-call | bytes 4194304 | tf_op jit(solution)/shard_map/pick/pallas_call | solution.py:368
  (2 shorter events, 0.1 us)
Async XLA Ops:
  0.6 19.9 %copy-start.1 = (bf16[128,512]{1,0:T(8,128)(2,1)S(1)}, bf16[128,512]{1,0:T(8,128)(2,1)}, u32[]{:S(2)}) copy-start(bf16[128,512]{1,0:T(8,128)(2,1)} %param.7) | copy-start | bytes 393220
  22.1 26.9 %copy-start.2 = (s32[1,16,1]{1,2,0:T(1,128)S(1)}, s32[1,16,1]{1,2,0:T(1,128)}, u32[]{:S(2)}) copy-start(s32[1,16,1]{1,2,0:T(1,128)} %param.9) | copy-start | bytes 196
  22.1 33.4 %all-to-all-start.1 = ((bf16[16,128,512]{2,1,0:T(8,128)(2,1)}), bf16[16,128,512]{2,1,0:T(8,128)(2,1)S(1)}, u32[]{:S(2)}, u32[]{:S(2)}) async-start(bf16[16,128,512]{2,1,0:T(8,128)(2,1)} %broadcast_in_dim.40), calls=%async_computation.1 | async-start | bytes 4194304 | tf_op jit(solution)/shard_map/all_to_all | solution.py:417
  25.9 14.7 %collective-permute-start.1 = (bf16[16,128,128]{2,1,0:T(8,128)(2,1)S(1)}, bf16[16,128,128]{2,1,0:T(8,128)(2,1)S(1)}, u32[]{:S(2)}, u32[]{:S(2)}) collective-permute-start(bf16[16,128,128]{2,1,0:T(8,128)(2,1)S(1)} %all_to_all.20.refs_0_), channel_id=1, source_target_pairs={{0,32},{32,64},{64,96},{96,0},{1,33},{33,65},{65,97},{97,1},{2,34}... | collective-permute-start | bytes 1572872 | tf_op jit(solution)/shard_map/ppermute | solution.py:382
  27.9 12.8 %collective-permute-start.3 = (bf16[16,128,128]{2,1,0:T(8,128)(2,1)S(1)}, bf16[16,128,128]{2,1,0:T(8,128)(2,1)}, u32[]{:S(2)}, u32[]{:S(2)}) collective-permute-start(bf16[16,128,128]{2,1,0:T(8,128)(2,1)S(1)} %all_to_all.20.refs_0_), channel_id=1, source_target_pairs={{0,96},{32,0},{64,32},{96,64},{1,97},{33,1},{65,33},{97,65},{2,98}... | collective-permute-start | bytes 1572872 | tf_op jit(solution)/shard_map/ppermute | solution.py:382
  40.7 7.7 %collective-permute-start.5 = (bf16[8,128,128]{2,1,0:T(8,128)(2,1)S(1)}, bf16[8,128,128]{2,1,0:T(8,128)(2,1)S(1)}, u32[]{:S(2)}, u32[]{:S(2)}) collective-permute-start(bf16[8,128,128]{2,1,0:T(8,128)(2,1)S(1)} %slice.8), channel_id=1, source_target_pairs={{0,32},{32,64},{64,96},{96,0},{1,33},{33,65},{65,97},{97,1},{2,34}... | collective-permute-start | bytes 786440 | tf_op jit(solution)/shard_map/ppermute | solution.py:382
  41.8 7.2 %collective-permute-start.6 = (bf16[8,128,128]{2,1,0:T(8,128)(2,1)S(1)}, bf16[8,128,128]{2,1,0:T(8,128)(2,1)}, u32[]{:S(2)}, u32[]{:S(2)}) collective-permute-start(bf16[8,128,128]{2,1,0:T(8,128)(2,1)S(1)} %slice.9), channel_id=1, source_target_pairs={{0,96},{32,0},{64,32},{96,64},{1,97},{33,1},{65,33},{97,65},{2,98}... | collective-permute-start | bytes 786440 | tf_op jit(solution)/shard_map/ppermute | solution.py:382
  45.0 4.9 %collective-permute-start = (bf16[16,128,128]{2,1,0:T(8,128)(2,1)S(1)}, bf16[16,128,128]{2,1,0:T(8,128)(2,1)}, u32[]{:S(2)}, u32[]{:S(2)}) collective-permute-start(bf16[16,128,128]{2,1,0:T(8,128)(2,1)S(1)} %all_to_all.20.refs_0_), channel_id=1, source_target_pairs={{0,16},{16,0},{1,17},{17,1},{2,18},{18,2},{3,19},{19,3},{4,20},{20... | collective-permute-start | bytes 1572872 | tf_op jit(solution)/shard_map/ppermute | solution.py:386
  45.0 5.8 %collective-permute-start.2 = (bf16[16,128,128]{2,1,0:T(8,128)(2,1)S(1)}, bf16[16,128,128]{2,1,0:T(8,128)(2,1)}, u32[]{:S(2)}, u32[]{:S(2)}) collective-permute-start(bf16[16,128,128]{2,1,0:T(8,128)(2,1)S(1)} %collective-permute-done.1.refs_2_), channel_id=1, source_target_pairs={{0,16},{16,0},{1,17},{17,1},{2,18},{18,2},{3,19},{19,3},{4,20},{20... | collective-permute-start | bytes 1572872 | tf_op jit(solution)/shard_map/ppermute | solution.py:386
  45.6 5.3 %collective-permute-start.4 = (bf16[16,128,128]{2,1,0:T(8,128)(2,1)}, bf16[16,128,128]{2,1,0:T(8,128)(2,1)}, u32[]{:S(2)}, u32[]{:S(2)}) collective-permute-start(bf16[16,128,128]{2,1,0:T(8,128)(2,1)} %collective-permute-done.3.refs_4_), channel_id=1, source_target_pairs={{0,16},{16,0},{1,17},{17,1},{2,18},{18,2},{3,19},{19,3},{4,20},{20... | collective-permute-start | bytes 1572872 | tf_op jit(solution)/shard_map/ppermute | solution.py:386
  48.3 1.7 %collective-permute-start.7 = (bf16[8,128,128]{2,1,0:T(8,128)(2,1)S(1)}, bf16[8,128,128]{2,1,0:T(8,128)(2,1)}, u32[]{:S(2)}, u32[]{:S(2)}) collective-permute-start(bf16[8,128,128]{2,1,0:T(8,128)(2,1)S(1)} %collective-permute-done.5.refs_6_), channel_id=1, source_target_pairs={{0,16},{16,0},{1,17},{17,1},{2,18},{18,2},{3,19},{19,3},{4,20},{20... | collective-permute-start | bytes 786440 | tf_op jit(solution)/shard_map/ppermute | solution.py:386
  48.9 1.9 %collective-permute-start.8 = (bf16[8,128,128]{2,1,0:T(8,128)(2,1)}, bf16[8,128,128]{2,1,0:T(8,128)(2,1)}, u32[]{:S(2)}, u32[]{:S(2)}) collective-permute-start(bf16[8,128,128]{2,1,0:T(8,128)(2,1)} %collective-permute-done.6.refs_7_), channel_id=1, source_target_pairs={{0,16},{16,0},{1,17},{17,1},{2,18},{18,2},{3,19},{19,3},{4,20},{20... | collective-permute-start | bytes 786440 | tf_op jit(solution)/shard_map/ppermute | solution.py:386
  60.4 34.0 %all-to-all-start.2 = ((bf16[16,2,64,512]{3,2,1,0:T(8,128)(2,1)}), bf16[16,2,64,512]{3,2,1,0:T(8,128)(2,1)S(1)}, u32[]{:S(2)}, u32[]{:S(2)}) async-start(bf16[16,2,64,512]{3,2,1,0:T(8,128)(2,1)} %bitcast.29), calls=%async_computation.2 | async-start | bytes 4194304 | tf_op jit(solution)/shard_map/all_to_all | solution.py:431
  94.3 4.8 %copy-start = (bf16[16,2,64,512]{3,2,1,0:T(8,128)(2,1)}, bf16[16,2,64,512]{3,2,1,0:T(8,128)(2,1)S(1)}, u32[]{:S(2)}) copy-start(bf16[16,2,64,512]{3,2,1,0:T(8,128)(2,1)S(1)} %all-to-all-done.2.grads) | copy-start | bytes 6291460
  99.1 36.9 %all-to-all-start.3 = ((bf16[16,2,64,512]{3,2,1,0:T(8,128)(2,1)}), bf16[16,2,64,512]{3,2,1,0:T(8,128)(2,1)S(1)}, u32[]{:S(2)}, u32[]{:S(2)}) async-start(bf16[16,2,64,512]{3,2,1,0:T(8,128)(2,1)} %directions.1), calls=%async_computation.3 | async-start | bytes 4194304 | tf_op jit(solution)/shard_map/all_to_all | solution.py:436
